TPU v7x, 32 devices: a whole 2x2x4 slice. The times are simulated.
32 devices in a mesh: section: 2 (over y), seq: 2 (over x), dp: 8 (over z, core).
Axes of the slice: x: 2, y: 2, z: 4, core: 2. Of those that a mesh axis runs over, the one named last changes fastest.
Arguments:
- layer_input: bfloat16 [2, 2, 8, 1024, 512], P('section', None, 'dp', 'seq'), may hold values from -6 to 6
- segment_ids: int32 [2, 2, 8, 1024], P('section', None, 'dp', 'seq'), may hold values from 0 to 3, as said below
- attn_qkv: bfloat16 [2, 512, 1536], P('section'), may hold values from -0.25 to 0.25
- attn_out: bfloat16 [2, 512, 512], P('section'), may hold values from -2 to 2
- ffn_in: bfloat16 [2, 512, 2048], P('section'), may hold values from -0.25 to 0.25
- ffn_out: bfloat16 [2, 2048, 512], P('section'), may hold values from -0.1875 to 0.1875
- norm_gain: float32 [2, 2, 512], P('section'), may hold values from 0.25 to 1.75
- cross_query: bfloat16 [512, 512], replicated, may hold values from -0.25 to 0.25
- cross_pair: bfloat16 [512, 1024], replicated, may hold values from -0.25 to 0.25
- cross_out: bfloat16 [512, 512], replicated, may hold values from -2 to 2
- cross_gain: float32 [512], replicated, may hold values from 0.25 to 1.75
- out_cotangent: bfloat16 [2, 8, 1024, 512], P(None, 'dp', 'seq'), may hold values from -6 to 6
Outputs:
- layer_output: bfloat16 [2, 2, 8, 1024, 512], P('section', None, 'dp', 'seq')
- input_grad: float32 [2, 2, 8, 1024, 512], P('section', None, 'dp', 'seq')
- grad_attn_qkv: float32 [2, 512, 1536], P('section')
- grad_attn_out: float32 [2, 512, 512], P('section')
- grad_ffn_in: float32 [2, 512, 2048], P('section')
- grad_ffn_out: float32 [2, 2048, 512], P('section')
- grad_norm_gain: float32 [2, 2, 512], P('section')
- grad_cross_query: float32 [512, 512], replicated
- grad_cross_pair: float32 [512, 1024], replicated
- grad_cross_out: float32 [512, 512], replicated
- grad_cross_gain: float32 [512], replicated
Inputs may be any that keep to these rules, and one draw needn't show every extreme that they name: `segment_ids`: along a row the numbers never fall and rise by one where a document starts. The source side (index 0) and the target side (index 1) of a row hold the same number of documents: 4 in every row except one of the 2 rows that one index of dp holds, which is a single document on both sides.
All inputs are finite; a program needn't handle non-finite values.
Results may differ from a plain program's by a relative error of at most 0.033.
Values may be sent and summed in bfloat16 or wider, within the bound.
No kernel may reach another device: no remote copies, remote signals or barrier semaphores. Data moves between devices by JAX's collectives and lax.ppermute only.
A program may use at most 320 MiB of HBM per device.

v0:
```python
import types

import jax
import jax.numpy as jnp
from jax import lax
from jax.experimental import pallas as pl
from jax.experimental.pallas import tpu as pltpu
from jax.sharding import PartitionSpec as P

HEADS = 8
TILE = 256
LANES = 128
CHUNK = 512

f32 = jnp.float32
bf16 = jnp.bfloat16
negative_big = -1e30
epsilon = 1e-05


def dot(left, right):
    return lax.dot_general(left, right, (((1,), (0,)), ((), ())), preferred_element_type=f32)


def dot_nt(left, right):
    return lax.dot_general(left, right, (((1,), (1,)), ((), ())), preferred_element_type=f32)


def dot_tn(left, right):
    return lax.dot_general(left, right, (((0,), (0,)), ((), ())), preferred_element_type=f32)


def standardize(values):
    center = values - jnp.mean(values, axis=-1, keepdims=True)
    inverse = lax.rsqrt(jnp.mean(center * center, axis=-1, keepdims=True) + epsilon)
    return center * inverse, inverse


def standardize_back(grad_out, standard, gain_row, inverse):
    scaled = grad_out * gain_row
    grad_in = inverse * (
        scaled
        - jnp.mean(scaled, axis=-1, keepdims=True)
        - standard * jnp.mean(scaled * standard, axis=-1, keepdims=True)
    )
    return grad_in, jnp.sum(grad_out * standard, axis=0, keepdims=True)


class Copies:
    def __init__(self, sems):
        self.sems = sems
        self.used = 0

    def start(self, source, target):
        copy = pltpu.make_async_copy(source, target, self.sems.at[self.used])
        self.used += 1
        copy.start()
        return copy


def wait_all(copies):
    for copy in copies:
        copy.wait()


def spread_pairs(target, source, factor, pairs):
    tiles = target.shape[1]
    half = lax.broadcasted_iota(jnp.int32, (TILE, LANES), 1) < LANES // 2
    first = jnp.where(half, factor, 0.0).astype(bf16)
    second = jnp.where(half, 0.0, factor).astype(bf16)
    for tile in range(tiles):
        for pair in pairs:
            block = source[tile * TILE : (tile + 1) * TILE, pair * LANES : (pair + 1) * LANES]
            target[pair, tile, :TILE, :] = block * first
            target[pair, tile, TILE:, :] = block * second


def turn_tiles(target, source, column, pairs):
    low, high = pairs[0] * LANES, (pairs[-1] + 1) * LANES
    for tile in range(target.shape[0]):
        block = source[tile * TILE : (tile + 1) * TILE, column + low : column + high]
        target[tile, low:high, :] = jnp.transpose(block)


def place_documents(r, copies):
    wait_all(copies)
    q_tiles = r.qd.shape[0]
    for part in range(3):
        row = r.docs[part].astype(f32)[0:1, :]
        for tile in range(q_tiles):
            piece = row[:, tile * TILE : (tile + 1) * TILE]
            slot = part * q_tiles + tile
            r.bounds[0, slot] = jnp.min(piece).astype(jnp.int32)
            r.bounds[1, slot] = jnp.max(piece).astype(jnp.int32)
            if part == 0:
                r.qd[tile] = jnp.broadcast_to(piece, (8, TILE))
        if part > 0:
            for start in range(0, row.shape[1], LANES):
                block = jnp.broadcast_to(row[:, start : start + LANES], (LANES, LANES))
                place = (part - 1) * row.shape[1] + start
                r.kdc[place : place + LANES, :] = jnp.transpose(block)


def load_documents(r, move, queries, own, other):
    rows = pl.ds(r.docs.shape[2], r.docs.shape[1])
    return [
        move.start(source.at[rows], r.docs.at[part])
        for part, source in enumerate((queries, own, other))
    ]


def tile_place(r, core, causal, q_tile, k_tile):
    q_tiles = r.qd.shape[0]
    length = q_tiles * TILE
    owner = jnp.where(k_tile < q_tiles, core, 1 - core)
    k_start = owner * length + lax.rem(k_tile, q_tiles) * TILE
    ahead = core * length + q_tile * TILE - k_start
    ahead = jnp.where(causal == 1, ahead, 2 * length * TILE)
    q_low, q_high = r.bounds[0, q_tile], r.bounds[1, q_tile]
    k_low, k_high = r.bounds[0, q_tiles + k_tile], r.bounds[1, q_tiles + k_tile]
    active = (q_low <= k_high) & (k_low <= q_high) & (ahead > -TILE)
    whole = (q_low == k_high) & (k_low == q_high) & (ahead >= TILE)
    return active, whole, ahead


def each_tile(place, body):
    active, whole, ahead = place
    pl.when(active & jnp.logical_not(whole))(lambda: body(ahead))
    pl.when(whole)(lambda: body(None))


def fill_bias(r, q_tile, k_tile, ahead):
    keys = r.kdc[pl.ds(pl.multiple_of(k_tile * TILE, TILE), TILE), :]
    shift = lax.broadcasted_iota(jnp.int32, (TILE, LANES), 0) - lax.broadcasted_iota(
        jnp.int32, (TILE, LANES), 1
    )
    queries = r.qd[q_tile]
    for start in range(0, TILE, LANES):
        same = keys == queries[0:1, start : start + LANES]
        allowed = same & (shift - start <= ahead)
        r.bias[:, start : start + LANES] = jnp.where(allowed, 0.0, negative_big)


def attention_forward(r, core, causal):
    pairs, q_tiles = r.qm.shape[:2]
    k_tiles = r.vt.shape[0]

    def one_query_tile(q_tile, carry):
        r.top[...] = jnp.full(r.top.shape, negative_big, f32)
        r.total[...] = jnp.zeros(r.total.shape, f32)
        r.turned[...] = jnp.zeros(r.turned.shape, f32)

        def one_key_tile(k_tile, inner):
            def one_tile(ahead):
                if ahead is not None:
                    fill_bias(r, q_tile, k_tile, ahead)
                rows = pl.ds(pl.multiple_of(k_tile * TILE, TILE), TILE)

                def raw(pair):
                    keys = r.kv[rows, pair * LANES : (pair + 1) * LANES]
                    return dot_nt(keys, r.qm[pair, q_tile])

                raw_next = raw(0)
                for pair in range(pairs):
                    scores = raw_next
                    if ahead is not None:
                        bias = r.bias[...]
                        scores = scores + jnp.concatenate([bias, bias], axis=1)
                    if pair + 1 < pairs:
                        raw_next = raw(pair + 1)
                    old_top = r.top[pair : pair + 1, :]
                    new_top = jnp.maximum(old_top, jnp.max(scores, axis=0, keepdims=True))
                    weights = jnp.exp(scores - new_top)
                    shrink = jnp.exp(old_top - new_top)
                    r.top[pair : pair + 1, :] = new_top
                    r.total[pair : pair + 1, :] = r.total[
                        pair : pair + 1, :
                    ] * shrink + jnp.sum(weights, axis=0, keepdims=True)
                    low = weights.astype(bf16)
                    for side in range(2):
                        span = slice(side * TILE, (side + 1) * TILE)
                        head = slice((2 * pair + side) * 64, (2 * pair + side + 1) * 64)
                        r.turned[head, :] = r.turned[head, :] * shrink[:, span] + dot(
                            r.vt[k_tile, head, :], low[:, span]
                        )

            each_tile(tile_place(r, core, causal, q_tile, k_tile), one_tile)
            return inner

        lax.fori_loop(0, k_tiles, one_key_tile, 0)
        for pair in range(pairs):
            total = r.total[pair : pair + 1, :]
            r.lse[q_tile, pair : pair + 1, :] = r.top[pair : pair + 1, :] + jnp.log(total)
            share = 1.0 / total
            for side in range(2):
                span = slice(side * TILE, (side + 1) * TILE)
                head = slice((2 * pair + side) * 64, (2 * pair + side + 1) * 64)
                r.turned[head, :] = r.turned[head, :] * share[:, span]
        rows = pl.ds(pl.multiple_of(q_tile * TILE, TILE), TILE)
        r.att[rows, :] = jnp.transpose(r.turned[...]).astype(bf16)
        return carry

    lax.fori_loop(0, q_tiles, one_query_tile, 0)


def row_products(r, grad_att, pairs):
    low, high = pairs[0] * LANES, (pairs[-1] + 1) * LANES
    for tile in range(r.qm.shape[1]):
        rows = slice(tile * TILE, (tile + 1) * TILE)
        product = jnp.transpose(
            grad_att[rows, low:high].astype(f32) * r.att[rows, low:high].astype(f32)
        )
        for pair in pairs:
            for side in range(2):
                head = (2 * pair + side) * 64 - low
                r.delta[tile, pair : pair + 1, side * TILE : (side + 1) * TILE] = jnp.sum(
                    product[head : head + 64, :], axis=0, keepdims=True
                )


def attention_backward(r, core, causal, pairs):
    q_tiles, k_tiles = r.qm.shape[1], r.kt.shape[0]
    width = r.kt.shape[1]
    low, high = pairs[0] * LANES, (pairs[-1] + 1) * LANES
    for start in (0, width):
        r.dkv[:, start + low : start + high] = jnp.zeros((r.dkv.shape[0], high - low), f32)

    def one_query_tile(q_tile, carry):
        r.turned[low:high, :] = jnp.zeros((high - low, TILE), f32)

        def one_key_tile(k_tile, inner):
            def one_tile(ahead):
                if ahead is not None:
                    fill_bias(r, q_tile, k_tile, ahead)
                rows = pl.ds(pl.multiple_of(k_tile * TILE, TILE), TILE)

                def raw(pair):
                    lanes = slice(pair * LANES, (pair + 1) * LANES)
                    lanes_v = slice(width + pair * LANES, width + (pair + 1) * LANES)
                    return (
                        dot_nt(r.kv[rows, lanes], r.qm[pair, q_tile]),
                        dot_nt(r.kv[rows, lanes_v], r.gm[pair, q_tile]),
                    )

                raw_next = raw(pairs[0])
                for pair in pairs:
                    scores, grad_probs = raw_next
                    if ahead is not None:
                        bias = r.bias[...]
                        scores = scores + jnp.concatenate([bias, bias], axis=1)
                    if pair < pairs[-1]:
                        raw_next = raw(pair + 1)
                    probs = jnp.exp(scores - r.lse[q_tile, pair : pair + 1, :])
                    grad_scores = probs * (grad_probs - r.delta[q_tile, pair : pair + 1, :])
                    probs_low = probs.astype(bf16)
                    grad_low = grad_scores.astype(bf16)
                    lanes = slice(pair * LANES, (pair + 1) * LANES)
                    lanes_v = slice(width + pair * LANES, width + (pair + 1) * LANES)
                    r.dkv[rows, lanes] += dot(grad_low, r.qm[pair, q_tile])
                    r.dkv[rows, lanes_v] += dot(probs_low, r.gm[pair, q_tile])
                    for side in range(2):
                        span = slice(side * TILE, (side + 1) * TILE)
                        head = slice((2 * pair + side) * 64, (2 * pair + side + 1) * 64)
                        r.turned[head, :] += dot(r.kt[k_tile, head, :], grad_low[:, span])

            each_tile(tile_place(r, core, causal, q_tile, k_tile), one_tile)
            return inner

        lax.fori_loop(0, k_tiles, one_key_tile, 0)
        rows = pl.ds(pl.multiple_of(q_tile * TILE, TILE), TILE)
        r.dq[rows, low:high] = jnp.transpose(r.turned[low:high, :]) * (64**-0.5)
        return carry

    lax.fori_loop(0, q_tiles, one_query_tile, 0)


def feed_forward(r, low):
    chunks = [slice(at, at + CHUNK) for at in range(0, r.w_in.shape[1], CHUNK)]
    upward_next = dot(low[...], r.w_in[:, chunks[0]])
    for place, span in enumerate(chunks):
        upward = upward_next
        if place + 1 < len(chunks):
            upward_next = dot(low[...], r.w_in[:, chunks[place + 1]])
        gate = jax.nn.sigmoid(upward)
        active = (upward * gate).astype(bf16)
        r.act[:, span] = active
        r.slope[:, span] = (gate + upward * gate * (1.0 - gate)).astype(r.slope.dtype)
        part = dot(active, r.w_down[span, :])
        if place:
            r.sum[...] += part
        else:
            r.sum[...] = part


def feed_backward(r):
    chunks = [slice(at, at + CHUNK) for at in range(0, r.w_in.shape[1], CHUNK)]
    active_next = dot_nt(r.down_grad[...], r.w_down[chunks[0], :])
    for place, span in enumerate(chunks):
        grad_active = active_next.astype(bf16)
        if place + 1 < len(chunks):
            active_next = dot_nt(r.down_grad[...], r.w_down[chunks[place + 1], :])
        grad_up = (grad_active.astype(f32) * r.slope[:, span].astype(f32)).astype(bf16)
        r.up_grad[:, span] = grad_up
        part = dot_nt(grad_up, r.w_in[:, span])
        if place:
            r.sum[...] += part
        else:
            r.sum[...] = part


def self_forward(r):
    length, width = r.unit1.shape
    decoder, core = r.meta[0], r.meta[1]
    move = Copies(r.sems)
    whole = pl.ds(0, length)
    documents = load_documents(r, move, r.x_own_h, r.x_own_h, r.x_other_h)
    early = [
        move.start(r.x_own_h.at[whole], r.x.at[whole]),
        move.start(r.x_other_h.at[whole], r.x.at[pl.ds(length, length)]),
        move.start(r.w_mixed_h, r.w_mixed),
    ]
    later = [
        move.start(r.w_out_h, r.w_out),
        move.start(r.w_in_h, r.w_in),
        move.start(r.w_down_h, r.w_down),
    ]
    place_documents(r, documents)
    wait_all(early)
    r.q[...] = dot(r.x[:length, :], r.w_mixed[:, :width]).astype(bf16)
    r.kv[...] = dot(r.x[...], r.w_mixed[:, width:]).astype(bf16)
    outs = [move.start(r.q, r.q_o), move.start(r.kv, r.kv_o)]
    pairs = range(width // LANES)
    spread_pairs(r.qm, r.q, 64**-0.5, pairs)
    turn_tiles(r.vt, r.kv, width, pairs)
    attention_forward(r, core, decoder)
    wait_all(later)
    outs += [move.start(r.att, r.att_o), move.start(r.lse, r.lse_o)]
    unit, inverse = standardize(r.x[:length, :].astype(f32) + dot(r.att[...], r.w_out[...]))
    r.unit1[...] = unit
    r.inv1[...] = jnp.broadcast_to(inverse, r.inv1.shape)
    r.first_low[...] = (unit * r.gains[0:1, :]).astype(bf16)
    outs += [
        move.start(r.unit1, r.unit1_o),
        move.start(r.inv1, r.inv1_o),
        move.start(r.first_low, r.first_low_o),
    ]

    @pl.when(decoder == 0)
    def _():
        feed_forward(r, r.first_low)
        late = [
            move.start(r.first_low, r.ffn_low_o),
            move.start(r.act, r.act_o),
            move.start(r.slope, r.slope_o),
        ]
        unit2, inverse2 = standardize(r.unit1[...] * r.gains[0:1, :] + r.sum[...])
        r.memory[:length, :] = (unit2 * r.gains[1:2, :]).astype(bf16)
        r.memory[length:, :] = r.docs[0]
        late += [move.start(r.memory, r.memory_o)]
        r.unit2[...] = unit2
        r.inv2[...] = jnp.broadcast_to(inverse2, r.inv2.shape)
        late += [move.start(r.unit2, r.unit2_o), move.start(r.inv2, r.inv2_o)]
        wait_all(late)

    wait_all(outs)


def cross_both_ways(r):
    length, width = r.unit1_h.shape
    core = r.meta[1]
    move = Copies(r.sems)
    whole = pl.ds(0, length)
    documents = load_documents(r, move, r.x_own_h, r.memory_own_h, r.memory_other_h)
    moves = [
        move.start(r.memory_own_h.at[whole], r.x.at[whole]),
        move.start(r.memory_other_h.at[whole], r.x.at[pl.ds(length, length)]),
        move.start(r.w_pair_h, r.w_pair),
        move.start(r.first_low_h, r.first_low),
        move.start(r.w_query_h, r.w_query),
    ]
    later = [
        move.start(r.unit1_h, r.unit1),
        move.start(r.w_cross_h, r.w_cross),
        move.start(r.w_in_h, r.w_in),
        move.start(r.w_down_h, r.w_down),
        move.start(r.cot_h.at[r.micro], r.cot),
    ]
    place_documents(r, documents)
    wait_all(moves)
    r.kv[...] = dot(r.x[...], r.w_pair[...]).astype(bf16)
    r.q[...] = dot(r.first_low[...], r.w_query[...]).astype(bf16)
    pairs = range(width // LANES)
    spread_pairs(r.qm, r.q, 64**-0.5, pairs)
    turn_tiles(r.vt, r.kv, width, pairs)
    turn_tiles(r.kt, r.kv, 0, pairs)
    attention_forward(r, core, 0)
    outs = [move.start(r.att, r.att_o)]
    wait_all(later)
    first = r.unit1[...] * r.gains[0:1, :]
    unit, inverse = standardize(first + dot(r.att[...], r.w_cross[...]))
    r.unit2[...] = unit
    r.inv2[...] = jnp.broadcast_to(inverse, r.inv2.shape)
    r.second_low[...] = (unit * r.cross_gain[...]).astype(bf16)
    outs += [move.start(r.second_low, r.ffn_low_o)]
    feed_forward(r, r.second_low)
    outs += [move.start(r.act, r.act_o)]
    unit3, inverse3 = standardize(r.unit2[...] * r.cross_gain[...] + r.sum[...])
    r.decoded[...] = (unit3 * r.gains[1:2, :]).astype(bf16)
    outs += [move.start(r.decoded, r.decoded_o)]
    grad_third, gain_late = standardize_back(
        r.cot[...].astype(f32), unit3, r.gains[1:2, :], inverse3
    )
    r.keep[...] = grad_third
    r.down_grad[...] = grad_third.astype(bf16)
    outs += [move.start(r.down_grad, r.down_grad_o)]
    feed_backward(r)
    outs += [move.start(r.up_grad, r.up_grad_o)]
    grad_sum, gain_cross = standardize_back(
        r.keep[...] + r.sum[...], r.unit2[...], r.cross_gain[...], r.inv2[:, 0:1]
    )
    r.gain_grads[...] = jnp.zeros(r.gain_grads.shape, f32)
    r.gain_grads[0:1, :] = gain_late
    r.gain_grads[1:2, :] = gain_cross
    r.keep[...] = grad_sum
    r.branch[...] = grad_sum.astype(bf16)
    outs += [move.start(r.gain_grads, r.gain_grads_o), move.start(r.branch, r.branch_o)]
    r.q[...] = dot_nt(r.branch[...], r.w_cross[...]).astype(bf16)
    spread_pairs(r.gm, r.q, 1.0, pairs)
    row_products(r, r.q, pairs)
    attention_backward(r, core, 0, pairs)
    r.dq_low[...] = r.dq[...].astype(bf16)
    r.keep[...] += dot_nt(r.dq_low[...], r.w_query[...])
    outs += [move.start(r.dq_low, r.dq_low_o), move.start(r.keep, r.grad_first_o)]
    r.dkv_low[...] = r.dkv[...].astype(bf16)
    outs += [move.start(r.dkv_low, r.dkv_o)]
    part = dot_nt(r.dkv_low[...], r.w_pair[...])
    r.part_other[...] = part[length:, :].astype(bf16)
    r.part_own[...] = part[:length, :]
    outs += [move.start(r.part_other, r.part_other_o), move.start(r.part_own, r.part_own_o)]
    wait_all(outs)


def feed_backward_alone(r):
    move = Copies(r.sems)
    early = [
        move.start(r.grad_memory_h, r.cot),
        move.start(r.unit2_h, r.unit2),
        move.start(r.inv2_h, r.inv2),
    ]
    later = [
        move.start(r.w_down_h, r.w_down),
        move.start(r.slope_h, r.slope),
        move.start(r.w_in_h, r.w_in),
    ]
    wait_all(early)
    grad_third, gain_late = standardize_back(
        r.cot[...].astype(f32), r.unit2[...], r.gains[1:2, :], r.inv2[:, 0:1]
    )
    r.gain_grads[...] = jnp.broadcast_to(gain_late, r.gain_grads.shape)
    r.keep[...] = grad_third
    r.down_grad[...] = grad_third.astype(bf16)
    outs = [move.start(r.down_grad, r.down_grad_o), move.start(r.gain_grads, r.gain_late_o)]
    wait_all(later)
    feed_backward(r)
    outs += [move.start(r.up_grad, r.up_grad_o)]
    r.keep[...] += r.sum[...]
    outs += [move.start(r.keep, r.grad_first_o)]
    wait_all(outs)


def self_backward(r, plan):
    r.micro, first, last = plan
    length, width = r.att_h.shape
    decoder, core = r.meta[0], r.meta[1]
    pairs = range(first, last)
    low, high = first * LANES, last * LANES
    move = Copies(r.sems)
    later = [
        move.start(r.q_h, r.q),
        move.start(r.kv_h, r.kv),
        move.start(r.att_h, r.att),
        move.start(r.lse_h, r.lse),
    ]
    if first == 0:
        early = [
            move.start(r.grad_first_h, r.keep),
            move.start(r.unit1_h, r.unit1),
            move.start(r.inv1_h, r.inv1),
            move.start(r.w_out_h, r.w_out),
        ]
    else:
        early = [move.start(r.grad_att_h, r.grad_att)]
    outs = []
    place_documents(r, load_documents(r, move, r.x_own_h, r.x_own_h, r.x_other_h))
    wait_all(early)
    if first == 0:
        grad_sum, gain_early = standardize_back(
            r.keep[...], r.unit1[...], r.gains[0:1, :], r.inv1[:, 0:1]
        )
        r.gain_grads[...] = jnp.broadcast_to(gain_early, r.gain_grads.shape)
        r.keep[...] = grad_sum
        r.branch[...] = grad_sum.astype(bf16)
        r.grad_att[...] = dot_nt(r.branch[...], r.w_out[...]).astype(bf16)
        outs += [move.start(r.gain_grads, r.gain_early_o), move.start(r.branch, r.branch_o)]
        if last < width // LANES:
            outs += [move.start(r.keep, r.grad_sum_o), move.start(r.grad_att, r.grad_att_o)]
    wait_all(later)
    if last == width // LANES:
        ends = [move.start(r.w_mixed_h, r.w_mixed)]
        if first > 0:
            ends += [
                move.start(r.grad_sum_h, r.keep),
                move.start(r.dq_h.at[:, pl.ds(0, low)], r.dq_low.at[:, pl.ds(0, low)]),
                move.start(r.dkv_h.at[:, pl.ds(0, low)], r.dkv_low.at[:, pl.ds(0, low)]),
                move.start(
                    r.dkv_h.at[:, pl.ds(width, low)], r.dkv_low.at[:, pl.ds(width, low)]
                ),
            ]
    spread_pairs(r.qm, r.q, 64**-0.5, pairs)
    turn_tiles(r.kt, r.kv, 0, pairs)
    spread_pairs(r.gm, r.grad_att, 1.0, pairs)
    row_products(r, r.grad_att, pairs)
    attention_backward(r, core, decoder, pairs)
    r.dq_low[:, low:high] = r.dq[:, low:high].astype(bf16)
    for start in (0, width):
        span = slice(start + low, start + high)
        r.dkv_low[:, span] = r.dkv[:, span].astype(bf16)
    if last == width // LANES:
        wait_all(ends)
        outs += [move.start(r.dq_low, r.dq_low_o), move.start(r.dkv_low, r.dkv_o)]
        r.keep[...] += dot_nt(r.dq_low[...], r.w_mixed[:, :width])
        part = dot_nt(r.dkv_low[...], r.w_mixed[:, width:])
        r.part_other[...] = part[length:, :].astype(bf16)
        r.keep[...] += part[:length, :]
        outs += [move.start(r.part_other, r.part_other_o), move.start(r.keep, r.part_own_o)]
    else:
        outs.append(move.start(r.dq_low.at[:, pl.ds(low, high - low)], r.dq_low_o.at[:, pl.ds(low, high - low)]))
        for start in (0, width):
            span = pl.ds(start + low, high - low)
            outs.append(move.start(r.dkv_low.at[:, span], r.dkv_o.at[:, span]))
    wait_all(outs)


def contract_blocks(r, plan):
    for core in range(2):

        @pl.when(r.meta[1] == core)
        def _(core=core):
            targets = [None] * 4
            for half in range(2):
                target = r.kept_o if half == core else r.sent_o
                targets[2 * half], targets[2 * half + 1] = target.at[0], target.at[1]
            order = (0, 1, 2, 3) if core else (2, 3, 0, 1)
            contract_in_order(r, plan(r), order, targets, Copies(r.sems))


def contract_in_order(r, blocks, order, targets, move):
    loads = dict()
    for slot in order:
        for buffer, sources, at in blocks[slot][1:]:
            if (id(buffer), at) not in loads:
                span = pl.ds(at * CHUNK, CHUNK)
                row = 0
                copies = []
                for source in sources:
                    rows = pl.ds(row, source.shape[0])
                    copies.append(move.start(source.at[:, span], buffer.at[rows, span]))
                    row += source.shape[0]
                loads[id(buffer), at] = copies
    outs = []
    held = dict()
    for slot in order:
        turn, (left, _, left_at), (right, _, right_at) = blocks[slot]
        wait_all(loads.pop((id(left), left_at), ()))
        wait_all(loads.pop((id(right), right_at), ()))
        if held.get(id(turn)) != left_at:
            for row in range(0, left.shape[0], CHUNK):
                block = left[row : row + CHUNK, left_at * CHUNK : (left_at + 1) * CHUNK]
                turn[:, row : row + CHUNK] = jnp.transpose(block)
            held[id(turn)] = left_at
        block = right[:, right_at * CHUNK : (right_at + 1) * CHUNK]
        r.blocks[slot] = dot(turn[:, : right.shape[0]], block).astype(bf16)
        outs.append(move.start(r.blocks.at[slot], targets[slot]))
    wait_all(outs)


def spread_pieces(r, targets):
    z = r.meta[3]
    group, height = r.own_h.shape[:2]
    rows = r.own_h.shape[2] // group
    for core in range(2):
        for x in range(2):

            @pl.when((r.meta[1] == core) & (r.meta[2] == x))
            def _(core=core, x=x):
                move = Copies(r.sems)
                parts = [
                    (r.own_h, core, x),
                    (r.own_x_h, core, 1 - x),
                    (r.other_h, 1 - core, x),
                    (r.other_x_h, 1 - core, 1 - x),
                ]
                loads = [
                    move.start(source, r.pieces.at[place])
                    for place, (source, _, _) in enumerate(parts)
                ]
                outs = []
                slot = 0
                gains = None
                for place, (_, half, side) in enumerate(parts):
                    loads[place].wait()
                    for step in range(group):
                        row = pl.multiple_of(lax.rem(z + (group - step), group) * rows, rows)
                        start = 0
                        for target in targets(r, 2 * half + side, row, rows):
                            r.wide[slot] = r.pieces[place, step, start : start + rows].astype(f32)
                            outs.append(move.start(r.wide.at[slot], target))
                            slot += 1
                            start += rows
                        if start < height:
                            extra = r.pieces[place, step, start:height].astype(f32)
                            gains = extra if gains is None else gains + extra
                r.gains_o[...] = gains[: r.gains_o.shape[0], :]
                wait_all(outs)


def launch(kernel, plan, side, scalars, small, large, outs, scratch, copies, work, previous=None, after=()):
    names = list(scalars) + list(small) + list(large)
    arrays = list(scalars.values()) + list(small.values()) + list(large.values())
    specs = (
        [pl.BlockSpec(memory_space=pltpu.SMEM)] * len(scalars)
        + [pl.BlockSpec(memory_space=pltpu.VMEM)] * len(small)
        + [pl.BlockSpec(memory_space=pl.ANY)] * len(large)
    )
    aliases = dict()
    for position, name in enumerate(outs):
        if previous and name in previous:
            aliases[len(arrays)] = position
            names.append("previous_" + name)
            arrays.append(previous[name])
            specs.append(pl.BlockSpec(memory_space=pl.ANY))
    for array in after:
        names.append("")
        arrays.append(array)
        specs.append(pl.BlockSpec(memory_space=pl.ANY))
    names += list(outs) + list(scratch) + ["sems"]

    def body(*refs):
        r = types.SimpleNamespace(**dict(zip(names, refs)))

        def run():
            if isinstance(plan, int):
                r.micro = plan
                kernel(r)
            else:
                kernel(r, plan)

        if side is None:
            run()
        else:
            pl.when(r.meta[0] == side)(run)

    results = pl.pallas_call(
        body,
        out_shape=[jax.ShapeDtypeStruct(*shape) for shape in outs.values()],
        in_specs=specs,
        out_specs=[
            pl.BlockSpec(memory_space=pltpu.VMEM if shape[0][0] < 8 else pl.ANY)
            for shape in outs.values()
        ],
        scratch_shapes=[
            pltpu.SMEM(*shape) if shape[1] == jnp.int32 else pltpu.VMEM(*shape)
            for shape in scratch.values()
        ]
        + [pltpu.SemaphoreType.DMA((copies,))],
        input_output_aliases=aliases,
        compiler_params=pltpu.CompilerParams(vmem_limit_bytes=58 * 1024 * 1024),
        cost_estimate=pl.CostEstimate(
            flops=work * 10**9, bytes_accessed=1 << 20, transcendentals=0
        ),
    )(*arrays)
    return types.SimpleNamespace(**dict(zip(outs, results)))


def attention_scratch(length, width):
    pairs, q_tiles, k_tiles = width // LANES, length // TILE, 2 * length // TILE
    return dict(
        q=((length, width), bf16),
        kv=((2 * length, 2 * width), bf16),
        qm=((pairs, q_tiles, 2 * TILE, LANES), bf16),
        kdc=((2 * length, LANES), f32),
        docs=((3, 16, width), bf16),
        qd=((length // TILE, 8, TILE), f32),
        bounds=((2, 3 * length // TILE), jnp.int32),
        bias=((TILE, TILE), f32),
        lse=((q_tiles, 8, 2 * TILE), f32),
        att=((length, width), bf16),
        turned=((width, TILE), f32),
    )


def forward_scratch(length, width):
    k_tiles = 2 * length // TILE
    return dict(
        vt=((k_tiles, width, TILE), bf16),
        top=((8, 2 * TILE), f32),
        total=((8, 2 * TILE), f32),
    )


def backward_scratch(length, width):
    pairs, q_tiles, k_tiles = width // LANES, length // TILE, 2 * length // TILE
    return dict(
        kt=((k_tiles, width, TILE), bf16),
        gm=((pairs, q_tiles, 2 * TILE, LANES), bf16),
        delta=((q_tiles, 8, 2 * TILE), f32),
        dkv=((2 * length, 2 * width), f32),
        dq=((length, width), f32),
        dkv_low=((2 * length, 2 * width), bf16),
        part_other=((length, width), bf16),
        dq_low=((length, width), bf16),
    )


def for_sending(shard):

    def short(part):
        return part.astype(jnp.bfloat16) if part.dtype == jnp.float32 else part

    return jax.tree.map(short, shard)


def from_behind(block, axis, distance):
    devices = range(lax.axis_size(axis))
    route = [(i - distance, i) for i in devices if i - distance in devices]
    return lax.ppermute(block, axis, route)


def from_root(shard, axis, root):
    mine = lax.axis_index(axis) == root
    return lax.psum(jnp.where(mine, shard, jnp.zeros_like(shard)), axis)


def matmul(left_side, right_side):
    return jnp.einsum("rsd,de->rse", left_side, right_side, preferred_element_type=jnp.float32)


def matmul_back(left_side, right_side):
    return jnp.einsum("rse,de->rsd", left_side, right_side, preferred_element_type=jnp.float32)


def contract(left_side, right_side):
    return jnp.einsum("rsd,rse->de", left_side, right_side, preferred_element_type=jnp.float32)


def normalize(values, gain_row):
    center = values - jnp.mean(values, axis=-1, keepdims=True)
    inverse = lax.rsqrt(jnp.mean(center * center, axis=-1, keepdims=True) + epsilon)
    standard = center * inverse
    return (standard * gain_row, standard, inverse)


def normalize_back(grad_out, standard, gain_row, inverse):
    scaled = grad_out * gain_row
    grad_in = inverse * (
        scaled
        - jnp.mean(scaled, axis=-1, keepdims=True)
        - standard * jnp.mean(scaled * standard, axis=-1, keepdims=True)
    )
    return (grad_in, jnp.sum(grad_out * standard, axis=(0, 1)))


def allowed_mask(query_docs, key_docs, query_place, key_place, causal):
    same_doc = query_docs[:, :, None] == key_docs[:, None, :]
    earlier = query_place[:, None] >= key_place[None, :]
    return (same_doc & (earlier | jnp.logical_not(causal)))[:, None]


def attend(queries, keys_local, values_local, query_docs, key_docs, causal, is_cross):
    rows_here, shard_len, model_width = queries.shape
    head_dim = model_width // HEADS
    score_scale = head_dim ** (-0.5)
    query_place = lax.axis_index("seq") * shard_len + jnp.arange(shard_len)
    query_heads = queries.reshape(rows_here, shard_len, HEADS, head_dim)

    def absorb(state_tuple, pieces):
        running_top, running_total, running_sum = state_tuple
        key_piece, value_piece, doc_piece = pieces
        piece_len = key_piece.shape[1]
        raw_scores = jnp.einsum(
            "rqhd,rkhd->rhqk",
            query_heads,
            key_piece.reshape(rows_here, piece_len, HEADS, head_dim),
            preferred_element_type=jnp.float32,
        )
        allowed = allowed_mask(query_docs, doc_piece, query_place, jnp.arange(piece_len), causal)
        scores = jnp.where(allowed, raw_scores * score_scale, negative_big)
        new_top = jnp.maximum(running_top, jnp.max(scores, axis=-1))
        weights = jnp.where(allowed, jnp.exp(scores - new_top[..., None]), 0.0)
        new_total = jnp.sum(weights, axis=-1)
        product = jnp.einsum(
            "rhqk,rkhd->rhqd",
            weights.astype(jnp.bfloat16),
            value_piece.reshape(rows_here, piece_len, HEADS, head_dim),
            preferred_element_type=jnp.float32,
        )
        return (new_top, new_total, product)

    init_state = (
        jnp.full((rows_here, HEADS, shard_len), negative_big, jnp.float32),
        jnp.zeros((rows_here, HEADS, shard_len), jnp.float32),
        jnp.zeros((rows_here, HEADS, shard_len, head_dim), jnp.float32),
    )
    if is_cross:
        final_top, final_total, final_sum = absorb(
            init_state,
            (
                lax.all_gather(keys_local, "seq", axis=1, tiled=True),
                lax.all_gather(values_local, "seq", axis=1, tiled=True),
                lax.all_gather(for_sending(key_docs), "seq", axis=1, tiled=True),
            ),
        )
    else:
        final_top, final_total, final_sum = absorb(
            init_state,
            (
                lax.all_gather(keys_local, "seq", axis=1, tiled=True),
                lax.all_gather(values_local, "seq", axis=1, tiled=True),
                lax.all_gather(key_docs, "seq", axis=1, tiled=True),
            ),
        )
    attended = (
        (final_sum / final_total[..., None])
        .transpose(0, 2, 1, 3)
        .reshape(rows_here, shard_len, model_width)
    )
    return (attended, final_top + jnp.log(final_total))


def attend_back(
    queries,
    keys_local,
    values_local,
    query_docs,
    key_docs,
    causal,
    log_total,
    grad_attended,
    is_cross,
):
    rows_here, shard_len, model_width = queries.shape
    head_dim = model_width // HEADS
    score_scale = head_dim ** (-0.5)
    query_place = lax.axis_index("seq") * shard_len + jnp.arange(shard_len)
    if is_cross:
        keys_full, values_full, docs_full = (
            lax.all_gather(keys_local, "seq", axis=1, tiled=True),
            lax.all_gather(values_local, "seq", axis=1, tiled=True),
            lax.all_gather(for_sending(key_docs), "seq", axis=1, tiled=True).astype(key_docs.dtype),
        )
    else:
        keys_full, values_full, docs_full = (
            lax.all_gather(keys_local, "seq", axis=1, tiled=True),
            lax.all_gather(values_local, "seq", axis=1, tiled=True),
            lax.all_gather(key_docs, "seq", axis=1, tiled=True),
        )
    full_len = keys_full.shape[1]
    query_heads = queries.reshape(rows_here, shard_len, HEADS, head_dim)
    key_heads = keys_full.reshape(rows_here, full_len, HEADS, head_dim)
    value_heads = values_full.reshape(rows_here, full_len, HEADS, head_dim)
    grad_heads = grad_attended.reshape(rows_here, shard_len, HEADS, head_dim)
    raw_scores = jnp.einsum(
        "rqhd,rkhd->rhqk", query_heads, key_heads, preferred_element_type=jnp.float32
    )
    allowed = allowed_mask(query_docs, docs_full, query_place, jnp.arange(full_len), causal)
    shifted = jnp.where(allowed, raw_scores * score_scale - log_total[..., None], negative_big)
    probs = jnp.where(allowed, jnp.exp(shifted), 0.0)
    grad_probs = jnp.einsum(
        "rqhd,rkhd->rhqk", grad_heads, value_heads, preferred_element_type=jnp.float32
    )
    delta = jnp.sum(probs * grad_probs, axis=-1)
    grad_scores = (probs * (grad_probs - delta[..., None]) * score_scale).astype(jnp.bfloat16)
    grad_queries = jnp.einsum(
        "rhqk,rkhd->rqhd", grad_scores, key_heads, preferred_element_type=jnp.float32
    ).reshape(rows_here, shard_len, model_width)
    probs_low = probs.astype(jnp.bfloat16)

    def key_terms(span):
        grad_keys = jnp.einsum(
            "rhqk,rqhd->krhd", grad_scores, query_heads, preferred_element_type=jnp.float32
        )
        grad_values = jnp.einsum(
            "rhqk,rqhd->krhd", probs_low, grad_heads, preferred_element_type=jnp.float32
        )
        return jnp.concatenate(
            [
                grad_keys.reshape(span, rows_here, model_width),
                grad_values.reshape(span, rows_here, model_width),
            ],
            axis=-1,
        )

    if is_cross:
        pair_terms = lax.psum_scatter(
            key_terms(shard_len * lax.axis_size("seq")).astype(jnp.bfloat16),
            "seq",
            scatter_dimension=0,
            tiled=True,
        ).astype(jnp.float32)
    else:
        pair_terms = lax.psum_scatter(
            key_terms(shard_len * lax.axis_size("seq")).astype(jnp.bfloat16),
            "seq",
            scatter_dimension=0,
            tiled=True,
        ).astype(jnp.float32)
    return (grad_queries, pair_terms.transpose(1, 0, 2))


def layer_forward(hidden_in, doc_own, memory, memory_docs, weights, is_decoder):
    (
        qkv_weight,
        out_weight,
        in_weight,
        down_weight,
        gains_pair,
        query_weight,
        pair_weight,
        cross_weight,
        cross_gains,
    ) = weights
    model_width = hidden_in.shape[-1]
    mixed = matmul(hidden_in, qkv_weight).astype(jnp.bfloat16)
    attended, self_lse = attend(
        mixed[..., :model_width],
        mixed[..., model_width : 2 * model_width],
        mixed[..., 2 * model_width :],
        doc_own,
        doc_own,
        is_decoder,
        False,
    )
    attended = attended.astype(jnp.bfloat16)
    first, first_unit, first_inv = normalize(
        hidden_in.astype(jnp.float32) + matmul(attended, out_weight), gains_pair[0]
    )
    first_low = first.astype(jnp.bfloat16)
    cross_queries = matmul(first_low, query_weight).astype(jnp.bfloat16)
    pair = matmul(memory, pair_weight).astype(jnp.bfloat16)
    cross_att, cross_lse = attend(
        cross_queries,
        pair[..., :model_width],
        pair[..., model_width:],
        doc_own,
        memory_docs,
        False,
        True,
    )
    cross_att = cross_att.astype(jnp.bfloat16)
    second_cross, second_unit, second_inv = normalize(
        first + matmul(cross_att, cross_weight), cross_gains
    )
    second = jnp.where(is_decoder, second_cross, first)
    second_low = second.astype(jnp.bfloat16)
    upward = matmul(second_low, in_weight)
    active = jax.nn.silu(upward).astype(jnp.bfloat16)
    result, third_unit, third_inv = normalize(second + matmul(active, down_weight), gains_pair[1])
    saved = {
        "mixed": mixed,
        "attended": attended,
        "self_lse": self_lse,
        "first_unit": first_unit,
        "first_inv": first_inv,
        "first_low": first_low,
        "cross_queries": cross_queries,
        "pair": pair,
        "cross_att": cross_att,
        "cross_lse": cross_lse,
        "second_unit": second_unit,
        "second_inv": second_inv,
        "second_low": second_low,
        "upward": upward,
        "active": active,
        "third_unit": third_unit,
        "third_inv": third_inv,
    }
    return (result, saved)


def layer_backward(
    grad_result, saved, hidden_in, doc_own, memory, memory_docs, weights, is_decoder
):
    (
        qkv_weight,
        out_weight,
        in_weight,
        down_weight,
        gains_pair,
        query_weight,
        pair_weight,
        cross_weight,
        cross_gains,
    ) = weights
    model_width = hidden_in.shape[-1]
    grad_third, grad_gain_late = normalize_back(
        grad_result, saved["third_unit"], gains_pair[1], saved["third_inv"]
    )
    down_grad = grad_third.astype(jnp.bfloat16)
    grad_down_w = contract(saved["active"], down_grad)
    grad_active = matmul_back(down_grad, down_weight).astype(jnp.bfloat16)
    sigmoid_up = jax.nn.sigmoid(saved["upward"])
    grad_upward = (
        grad_active.astype(jnp.float32)
        * (sigmoid_up + saved["upward"] * sigmoid_up * (1.0 - sigmoid_up))
    ).astype(jnp.bfloat16)
    grad_in_w = contract(saved["second_low"], grad_upward)
    grad_second = grad_third + matmul_back(grad_upward, in_weight)
    grad_cross_sum, grad_cross_gain = normalize_back(
        grad_second, saved["second_unit"], cross_gains, saved["second_inv"]
    )
    decoder_flag = is_decoder.astype(jnp.float32)
    grad_cross_sum = grad_cross_sum * decoder_flag
    grad_cross_gain = grad_cross_gain * decoder_flag
    cross_branch = grad_cross_sum.astype(jnp.bfloat16)
    grad_cross_w = contract(saved["cross_att"], cross_branch)
    grad_cross_att = matmul_back(cross_branch, cross_weight).astype(jnp.bfloat16)
    pair = saved["pair"]
    grad_cross_q, grad_pair = attend_back(
        saved["cross_queries"],
        pair[..., :model_width],
        pair[..., model_width:],
        doc_own,
        memory_docs,
        False,
        saved["cross_lse"],
        grad_cross_att,
        True,
    )
    grad_cross_q = grad_cross_q.astype(jnp.bfloat16)
    grad_pair = grad_pair.astype(jnp.bfloat16)
    grad_query_w = contract(saved["first_low"], grad_cross_q)
    grad_pair_w = contract(memory, grad_pair)
    grad_memory = matmul_back(grad_pair, pair_weight)
    grad_first = jnp.where(
        is_decoder, grad_cross_sum + matmul_back(grad_cross_q, query_weight), grad_second
    )
    grad_first_sum, grad_gain_early = normalize_back(
        grad_first, saved["first_unit"], gains_pair[0], saved["first_inv"]
    )
    self_branch = grad_first_sum.astype(jnp.bfloat16)
    grad_out_w = contract(saved["attended"], self_branch)
    grad_attended = matmul_back(self_branch, out_weight).astype(jnp.bfloat16)
    mixed = saved["mixed"]
    grad_queries, grad_pair_self = attend_back(
        mixed[..., :model_width],
        mixed[..., model_width : 2 * model_width],
        mixed[..., 2 * model_width :],
        doc_own,
        doc_own,
        is_decoder,
        saved["self_lse"],
        grad_attended,
        False,
    )
    grad_mixed = jnp.concatenate([grad_queries, grad_pair_self], axis=-1).astype(jnp.bfloat16)
    grad_qkv_w = contract(hidden_in, grad_mixed)
    grad_hidden = grad_first_sum + matmul_back(grad_mixed, qkv_weight)
    layer_grads = (
        grad_qkv_w,
        grad_out_w,
        grad_in_w,
        grad_down_w,
        jnp.stack([grad_gain_early, grad_gain_late]),
        grad_query_w,
        grad_pair_w,
        grad_cross_w,
        grad_cross_gain,
    )
    return (grad_hidden, grad_memory, layer_grads)


def any_rows(
    layer_input,
    segment_ids,
    attn_qkv,
    attn_out,
    ffn_in,
    ffn_out,
    norm_gain,
    cross_query,
    cross_pair,
    cross_out,
    cross_gain,
    out_cotangent,
):
    micro_count = layer_input.shape[1]
    section_index = lax.axis_index("section")
    is_decoder = section_index == 1
    weights = (
        attn_qkv[0],
        attn_out[0],
        ffn_in[0],
        ffn_out[0],
        norm_gain[0],
        cross_query,
        cross_pair,
        cross_out,
        cross_gain,
    )
    inputs_all = layer_input[0]
    docs_all = segment_ids[0]
    slot_ids = jnp.arange(micro_count)
    received = (jnp.zeros_like(inputs_all[0]), jnp.zeros_like(docs_all[0]))
    results = jnp.zeros_like(inputs_all)
    memories = []
    memory_doc_list = []
    for step_index in range(micro_count + 1):
        batch_index = step_index - section_index
        is_valid = (batch_index >= 0) & (batch_index < micro_count)
        chosen = jnp.clip(batch_index, 0, micro_count - 1)
        hidden_in = lax.dynamic_index_in_dim(inputs_all, chosen, 0, keepdims=False)
        doc_own = lax.dynamic_index_in_dim(docs_all, chosen, 0, keepdims=False)
        memory = received[0]
        memory_docs = jnp.where(is_valid & is_decoder, received[1], doc_own)
        memories.append(memory)
        memory_doc_list.append(memory_docs)
        result, saved = layer_forward(hidden_in, doc_own, memory, memory_docs, weights, is_decoder)
        low_result = result.astype(jnp.bfloat16)
        writing = (slot_ids == chosen) & is_valid
        results = jnp.where(writing[:, None, None, None], low_result[None], results)
        if step_index < micro_count:
            received = from_behind((low_result, doc_own), "section", 1)
    memory_stack = jnp.stack(memories)
    memory_doc_stack = jnp.stack(memory_doc_list)
    totals = tuple((jnp.zeros(weight.shape, jnp.float32) for weight in weights))
    input_grads = jnp.zeros(inputs_all.shape, jnp.float32)
    returned = jnp.zeros(inputs_all.shape[1:], jnp.float32)
    for step_index in range(micro_count + 1):
        batch_index = micro_count - step_index - section_index
        is_valid = (batch_index >= 0) & (batch_index < micro_count)
        chosen = jnp.clip(batch_index, 0, micro_count - 1)
        forward_step = jnp.clip(batch_index + section_index, 0, micro_count)
        hidden_in = lax.dynamic_index_in_dim(inputs_all, chosen, 0, keepdims=False)
        doc_own = lax.dynamic_index_in_dim(docs_all, chosen, 0, keepdims=False)
        memory = lax.dynamic_index_in_dim(memory_stack, forward_step, 0, keepdims=False)
        memory_docs = lax.dynamic_index_in_dim(memory_doc_stack, forward_step, 0, keepdims=False)
        discarded, saved = layer_forward(
            hidden_in, doc_own, memory, memory_docs, weights, is_decoder
        )
        cotangent = jnp.where(
            is_decoder,
            lax.dynamic_index_in_dim(out_cotangent, chosen, 0, keepdims=False).astype(jnp.float32),
            returned,
        )
        grad_hidden, grad_memory, layer_grads = layer_backward(
            cotangent, saved, hidden_in, doc_own, memory, memory_docs, weights, is_decoder
        )
        valid_flag = is_valid.astype(jnp.float32)
        totals = tuple(
            (running + valid_flag * fresh for running, fresh in zip(totals, layer_grads))
        )
        writing = (slot_ids == chosen) & is_valid
        input_grads = jnp.where(writing[:, None, None, None], grad_hidden[None], input_grads)
        if step_index < micro_count:
            returned = from_behind(grad_memory.astype(jnp.bfloat16), "section", -1).astype(
                grad_memory.dtype
            )
    group_sums = lax.psum(
        (
            totals[0],
            totals[1],
            totals[2],
            totals[3],
            totals[4],
            totals[5],
            totals[6],
            totals[7],
            totals[8],
        ),
        ("seq", "dp"),
    )
    section_sums = group_sums[:5]
    cross_sums = (
        from_root(group_sums[5].astype(jnp.bfloat16), "section", 1).astype(jnp.float32),
        from_root(group_sums[6].astype(jnp.bfloat16), "section", 1).astype(jnp.float32),
        from_root(group_sums[7].astype(jnp.bfloat16), "section", 1).astype(jnp.float32),
        from_root(group_sums[8].astype(jnp.bfloat16), "section", 1).astype(jnp.float32),
    )
    return (
        results[None],
        input_grads[None],
        section_sums[0][None],
        section_sums[1][None],
        section_sums[2][None],
        section_sums[3][None],
        section_sums[4][None],
        cross_sums[0],
        cross_sums[1],
        cross_sums[2],
        cross_sums[3],
    )


def split_rows(
    layer_input,
    segment_ids,
    attn_qkv,
    attn_out,
    ffn_in,
    ffn_out,
    norm_gain,
    cross_query,
    cross_pair,
    cross_out,
    cross_gain,
    out_cotangent,
):
    micros = layer_input.shape[1]
    length, width = layer_input.shape[3:]
    hidden = ffn_in.shape[-1]
    q_tiles = length // TILE
    group = lax.axis_size("dp") // 2
    axes = ("section", "seq", "dp")
    decoder = lax.axis_index("section") == 1
    flag = decoder.astype(jnp.int32)
    x = lax.axis_index("seq")
    core = lax.rem(lax.axis_index("dp"), 2)
    z = lax.axis_index("dp") // 2
    places = [(t, i, k, c) for t in range(2) for i in range(2) for k in range(group) for c in range(2)]

    def number(t, i, k, c):
        return ((t * 2 + i) * group + k) * 2 + c

    def send(values, target, section=None):
        route = [
            (number(*place), number(*target(*place)))
            for place in places
            if section in (None, place[0]) and target(*place)
        ]
        return lax.ppermute(values, axes, route)

    def to_core(t, i, k, c):
        return (t, i, k, 1 - c)

    def to_x(t, i, k, c):
        return (t, 1 - i, k, c)

    def to_row(t, i, k, c):
        return (t, c, k, i)

    def to_decoder(t, i, k, c):
        return (1, i, k, c) if t == 0 else None

    def to_encoder(t, i, k, c):
        return (0, i, k, c) if t == 1 else None

    def fence(values, *before):
        return lax.optimization_barrier((values,) + before)[0]

    def exchange(values):
        return send(values, to_core)

    low = ((length, width), bf16)
    wide = ((length, width), f32)
    marked = ((length + 16, width), bf16)
    both = ((2 * length, width), bf16)
    keys_all = ((2 * length, 2 * width), bf16)
    mixing = ((width, 3 * width), bf16)
    inner = ((length, hidden), bf16)
    lse = ((q_tiles, 8, 2 * TILE), f32)
    stat = ((length, LANES), f32)
    square = ((width, width), bf16)
    rising = ((width, hidden), bf16)
    falling = ((hidden, width), bf16)
    gain_rows = ((8, width), f32)

    meta = jnp.stack([flag, core, x, z]).astype(jnp.int32)
    numbers = segment_ids[0, :, 0].astype(bf16)
    padding = jnp.zeros((15, width), bf16)
    with_numbers = [
        jnp.concatenate([layer_input[0, micro, 0], numbers[micro][None], padding])
        for micro in range(micros)
    ]
    own = [send(with_numbers[0], to_row)]
    for micro in range(1, micros):
        own.append(send(fence(with_numbers[micro], own[-1]), to_row))
    other = [exchange(own[0])]

    plain = dict(meta=meta)
    small = dict(gains=norm_gain[0])
    forward, memories, memories_other = [], [], []
    for micro in range(micros):
        call = launch(
            self_forward,
            micro,
            None,
            plain,
            small,
            dict(
                x_own_h=own[micro],
                x_other_h=other[micro],
                w_mixed_h=attn_qkv[0],
                w_out_h=attn_out[0],
                w_in_h=ffn_in[0],
                w_down_h=ffn_out[0],
            ),
            dict(
                q_o=low,
                kv_o=keys_all,
                att_o=low,
                lse_o=lse,
                unit1_o=wide,
                inv1_o=stat,
                first_low_o=low,
                memory_o=marked,
                ffn_low_o=low,
                act_o=inner,
                slope_o=inner,
                unit2_o=wide,
                inv2_o=stat,
            ),
            dict(
                **attention_scratch(length, width),
                **forward_scratch(length, width),
                x=both,
                w_mixed=mixing,
                w_out=square,
                w_in=rising,
                w_down=falling,
                unit1=wide,
                inv1=stat,
                first_low=low,
                memory=marked,
                act=inner,
                slope=inner,
                unit2=wide,
                inv2=stat,
                sum=wide,
            ),
            28,
            26,
            after=(forward[0].lse_o,) if micro else (),
        )
        forward.append(call)
        memories.append(send(call.memory_o, to_decoder))
        if micro + 1 < micros:
            other.append(exchange(fence(own[micro + 1], call.lse_o)))

    for micro in range(micros):
        memories_other.append(exchange(fence(memories[micro], forward[-1].lse_o)))
    cotangent = send(fence(out_cotangent[:, 0], forward[0].lse_o), to_row)

    cross, grads_memory, made = [], [], []
    after = (forward[-1].lse_o,)
    for micro in range(micros):
        done = forward[micro]
        call = launch(
            cross_both_ways,
            micro,
            1,
            plain,
            dict(**small, cross_gain=cross_gain[None]),
            dict(
                x_own_h=own[micro],
                memory_own_h=memories[micro],
                memory_other_h=memories_other[micro],
                w_pair_h=cross_pair,
                first_low_h=done.first_low_o,
                unit1_h=done.unit1_o,
                w_query_h=cross_query,
                w_cross_h=cross_out,
                w_in_h=ffn_in[0],
                w_down_h=ffn_out[0],
                cot_h=cotangent,
            ),
            dict(
                att_o=low,
                ffn_low_o=low,
                act_o=inner,
                decoded_o=low,
                down_grad_o=low,
                up_grad_o=inner,
                gain_grads_o=gain_rows,
                branch_o=low,
                dq_low_o=low,
                dkv_o=keys_all,
                part_own_o=wide,
                part_other_o=low,
                grad_first_o=wide,
            ),
            dict(
                **attention_scratch(length, width),
                **forward_scratch(length, width),
                **backward_scratch(length, width),
                x=both,
                w_pair=((width, 2 * width), bf16),
                first_low=low,
                unit1=wide,
                w_query=square,
                w_cross=square,
                w_in=rising,
                w_down=falling,
                cot=low,
                unit2=wide,
                inv2=stat,
                second_low=low,
                act=inner,
                slope=inner,
                sum=wide,
                decoded=low,
                keep=wide,
                down_grad=low,
                up_grad=inner,
                gain_grads=gain_rows,
                branch=low,
                part_own=wide,
            ),
            36,
            44,
            dict(act_o=done.act_o, ffn_low_o=done.ffn_low_o),
            after,
        )
        cross.append(call)
        away = call.part_other_o
        if micro:
            away = fence(away, grads_memory[-1])
        total = call.part_own_o + exchange(away).astype(f32)
        made.append(total.astype(bf16))
        after = (made[micro],)
        grads_memory.append(send(made[micro], to_encoder))

    def backward_feed(micro, after):
        done, late = forward[micro], cross[micro]
        return launch(
            feed_backward_alone,
            micro,
            0,
            plain,
            dict(gains=norm_gain[0]),
            dict(
                grad_memory_h=grads_memory[micro],
                unit2_h=done.unit2_o,
                inv2_h=done.inv2_o,
                slope_h=done.slope_o,
                w_in_h=ffn_in[0],
                w_down_h=ffn_out[0],
            ),
            dict(gain_late_o=gain_rows, down_grad_o=low, up_grad_o=inner, grad_first_o=wide),
            dict(
                cot=low,
                unit2=wide,
                inv2=stat,
                slope=inner,
                w_in=rising,
                w_down=falling,
                gain_grads=gain_rows,
                keep=wide,
                down_grad=low,
                up_grad=inner,
                sum=wide,
            ),
            12,
            10,
            dict(
                down_grad_o=late.down_grad_o, up_grad_o=late.up_grad_o, grad_first_o=late.grad_first_o
            ),
            after,
        )

    def backward_self(micro, side, grad_first, previous=None, after=(), halfway=None):
        done = forward[micro]
        heads = width // LANES
        given = dict(
            x_own_h=own[micro],
            x_other_h=other[micro],
            q_h=done.q_o,
            kv_h=done.kv_o,
            att_h=done.att_o,
            lse_h=done.lse_o,
        )
        ahead = dict(
            grad_first_h=grad_first,
            unit1_h=done.unit1_o,
            inv1_h=done.inv1_o,
            w_out_h=attn_out[0],
        )
        makes = dict(dq_low_o=low, dkv_o=keys_all)
        makes_first = dict(gain_early_o=gain_rows, branch_o=low)
        makes_last = dict(part_own_o=wide, part_other_o=low)
        scratch = dict(
            **attention_scratch(length, width),
            **backward_scratch(length, width),
            w_out=square,
            w_mixed=mixing,
            unit1=wide,
            inv1=stat,
            keep=wide,
            branch=low,
            grad_att=low,
            gain_grads=gain_rows,
        )

        def part(first, last, large, outs, work, previous, after):
            return launch(
                self_backward,
                (micro, first, last),
                side,
                plain,
                small,
                dict(**given, **large),
                dict(**makes, **outs),
                scratch,
                28,
                work,
                previous,
                after,
            )

        if halfway is None:
            large = dict(**ahead, w_mixed_h=attn_qkv[0])
            outs = dict(**makes_first, **makes_last)
            return part(0, heads, large, outs, 22, previous, after)
        outs = dict(**makes_first, grad_sum_o=wide, grad_att_o=low)
        one = part(0, heads // 2, ahead, outs, 12, None, after)
        large = dict(
            w_mixed_h=attn_qkv[0],
            grad_sum_h=one.grad_sum_o,
            grad_att_h=one.grad_att_o,
            dq_h=one.dq_low_o,
            dkv_h=one.dkv_o,
        )
        two = part(heads // 2, heads, large, makes_last, 12, None, halfway(one))
        return types.SimpleNamespace(**{**vars(one), **vars(two)})

    def weight_grads(plan, side, arrays, scratch, after=()):
        blocks = ((2, width, width), bf16)
        call = launch(
            contract_blocks,
            plan,
            side,
            plain,
            dict(),
            arrays,
            dict(sent_o=blocks, kept_o=blocks),
            dict(**scratch, blocks=((4, width, width), bf16)),
            36,
            8,
            after=after,
        )
        return call.sent_o, call.kept_o

    def first_sums(halves, section=None):
        sent, kept = halves
        got = send(sent, to_core, section)

        def block(side):
            return sum(
                lax.dynamic_index_in_dim(part, side, 0, keepdims=False).astype(f32)
                for part in (kept, got)
            )

        return block(1 - x).astype(bf16), block(x)

    def middle_sums(sums, section=None):
        away, total = sums
        return (total + send(away, to_x, section).astype(f32)).astype(bf16)

    def last_sums(totals, *later):
        rows = width // group
        shares = jnp.concatenate([total.reshape(group, rows, width) for total in totals], axis=1)

        def share(step):
            return lax.dynamic_index_in_dim(shares, lax.rem(z + step, group), 0, keepdims=False)

        parts = [share(0)]
        for step in range(1, group):
            parts.append(send(share(step), along_z(step)))
        if later:
            parts = [fence(part, *later) for part in parts]
        return sum(part.astype(f32) for part in parts).astype(bf16)

    def along_z(step):
        return lambda t, i, k, c: (t, i, (k + step) % group, c)

    def gather_z(share):
        return [share] + [send(share, along_z(step)) for step in range(1, group)]

    def gain_block(rows):
        filled = jnp.concatenate([jnp.stack(rows), jnp.zeros((16 - len(rows), width), f32)])
        return filled.astype(bf16)

    def spread(targets, own, own_x, outs, parts):
        return launch(
            spread_pieces,
            targets,
            None,
            plain,
            dict(),
            dict(own_h=own, own_x_h=own_x, other_h=exchange(own), other_x_h=exchange(own_x)),
            outs,
            dict(
                pieces=((4,) + own.shape, bf16),
                wide=((4 * group * parts, width // group, width), f32),
            ),
            8 + 4 * group * parts,
            5,
        )

    tokens, all_tokens = micros * length, 2 * micros * length
    turn, turn_all = ((width, tokens), bf16), ((width, all_tokens), bf16)
    narrow, narrow_all = ((tokens, width), bf16), ((all_tokens, width), bf16)
    pair_all = ((all_tokens, 2 * width), bf16)
    deep = ((tokens, hidden), bf16)

    def part_of(buffer, *sources):
        return lambda column: (buffer, sources, column)

    def key_rows(buffer, sources):
        first, second = pl.ds(0, length), pl.ds(length, length)
        return part_of(buffer, *[source.at[rows] for rows in (first, second) for source in sources])

    def cross_plan(r):
        rows = pl.ds(0, length)
        low_part = part_of(r.low, r.low0_h, r.low1_h)
        att_part = part_of(r.att, r.att0_h, r.att1_h)
        dq_part = part_of(r.dq, r.dq0_h, r.dq1_h)
        branch_part = part_of(r.branch, r.branch0_h, r.branch1_h)
        sources = (r.mem0_h, r.mem1_h, r.mem2_h, r.mem3_h)
        mem_part = part_of(r.mem, *[source.at[rows] for source in sources])
        pair_part = key_rows(r.pair, (r.pair0_h, r.pair1_h))
        return [
            (r.turn, low_part(0), dq_part(0)),
            (r.turn_att, att_part(0), branch_part(0)),
            (r.turn_all, mem_part(0), pair_part(0)),
            (r.turn_all, mem_part(0), pair_part(1)),
        ]

    def rising_plan(r):
        low_part = part_of(r.low, r.low0_h, r.low1_h)
        up_part = part_of(r.up, r.up0_h, r.up1_h)
        return [(r.turn, low_part(0), up_part(block)) for block in range(4)]

    def falling_plan(r):
        act_part = part_of(r.act, r.act0_h, r.act1_h)
        down_part = part_of(r.down, r.down0_h, r.down1_h)
        return [(r.turn, act_part(block), down_part(0)) for block in range(4)]

    def self_plan(r):
        rows = pl.ds(0, length)
        sources = (r.x0_h, r.x1_h, r.x2_h, r.x3_h)
        x_part = part_of(r.x, *[source.at[rows] for source in sources])
        dq_part = part_of(r.dq, r.dq0_h, r.dq1_h)
        pair_part = key_rows(r.pair, (r.pair0_h, r.pair1_h))
        att_part = part_of(r.att, r.att0_h, r.att1_h)
        branch_part = part_of(r.branch, r.branch0_h, r.branch1_h)
        return [
            (r.turn_all, x_part(0), dq_part(0)),
            (r.turn_all, x_part(0), pair_part(0)),
            (r.turn_all, x_part(0), pair_part(1)),
            (r.turn, att_part(0), branch_part(0)),
        ]

    last = micros - 1
    feeds, ends = [None] * micros, [None] * micros
    cross_halves = weight_grads(
        cross_plan,
        1,
        dict(
            low0_h=forward[0].first_low_o,
            low1_h=forward[1].first_low_o,
            dq0_h=cross[0].dq_low_o,
            dq1_h=cross[1].dq_low_o,
            att0_h=cross[0].att_o,
            att1_h=cross[1].att_o,
            branch0_h=cross[0].branch_o,
            branch1_h=cross[1].branch_o,
            mem0_h=memories[0],
            mem1_h=memories[1],
            mem2_h=memories_other[0],
            mem3_h=memories_other[1],
            pair0_h=cross[0].dkv_o,
            pair1_h=cross[1].dkv_o,
        ),
        dict(
            low=narrow,
            dq=narrow,
            att=narrow,
            branch=narrow,
            mem=narrow_all,
            pair=pair_all,
            turn=turn,
            turn_att=turn,
            turn_all=turn_all,
        ),
        (made[last],),
    )
    cross_sums = first_sums(cross_halves, 1)
    results = jnp.stack(
        [
            jnp.where(decoder, call.decoded_o, done.memory_o[:length])
            for call, done in zip(cross, forward)
        ]
    )
    results = send(results, to_row)
    latest = made[last]

    def part_sum(micro, *before):
        end = ends[micro]
        away = fence(end.part_other_o, *before)
        total = (end.part_own_o + exchange(away).astype(f32)).astype(bf16)
        return total, send(total, to_row)

    steps = []
    for micro in range(last):
        feeds[micro] = backward_feed(micro, (latest,))
        first = feeds[micro].grad_first_o
        ends[micro] = backward_self(micro, 0, first)
        ends[micro] = backward_self(micro, 1, first, vars(ends[micro]), (cross_sums[0], grads_memory[last]))
        cross_total = middle_sums(cross_sums, 1)
        steps.append(part_sum(micro, cross_total))
        latest = ends[micro].gain_early_o
    feeds[last] = backward_feed(last, (latest,))

    rising_halves = weight_grads(
        rising_plan,
        None,
        dict(
            low0_h=cross[0].ffn_low_o,
            low1_h=cross[1].ffn_low_o,
            up0_h=feeds[0].up_grad_o,
            up1_h=feeds[1].up_grad_o,
        ),
        dict(low=narrow, up=deep, turn=turn),
        (results,) + tuple(step[0] for step in steps),
    )
    rising_sums = first_sums(rising_halves)
    rising_total = middle_sums(rising_sums)
    falling_halves = weight_grads(
        falling_plan,
        None,
        dict(
            act0_h=cross[0].act_o,
            act1_h=cross[1].act_o,
            down0_h=feeds[0].down_grad_o,
            down1_h=feeds[1].down_grad_o,
        ),
        dict(act=deep, down=narrow, turn=turn),
        (rising_sums[0],),
    )
    falling_sent = fence(falling_halves[0], rising_total)
    falling_sums = first_sums((falling_sent, falling_halves[1]))
    falling_total = middle_sums(falling_sums)
    shares = []

    third = sum(call.gain_grads_o[1] for call in cross)

    def halfway(one):
        both = last_sums((rising_total, cross_total), one.gain_early_o)
        rows = width // group
        found = jnp.concatenate([both[rows:], gain_block([third])])
        shares.extend([both[:rows], found, send(found, to_encoder)])
        return (both, falling_total)

    ends[last] = backward_self(
        last,
        None,
        feeds[last].grad_first_o,
        None,
        (falling_sums[0],),
        halfway,
    )
    finished = ends[last].part_own_o
    falling_share = last_sums((falling_total,), ends[last].gain_early_o, finished)
    rising_share, found, arrived = shares
    cross_share = jnp.where(decoder, found, fence(arrived, finished))
    one_own = gather_z(jnp.concatenate([rising_share, falling_share, cross_share]))
    steps.append(part_sum(last, falling_share, arrived, steps[0][1]))

    self_halves = weight_grads(
        self_plan,
        None,
        dict(
            x0_h=own[0],
            x1_h=own[1],
            x2_h=other[0],
            x3_h=other[1],
            dq0_h=ends[0].dq_low_o,
            dq1_h=ends[1].dq_low_o,
            pair0_h=ends[0].dkv_o,
            pair1_h=ends[1].dkv_o,
            att0_h=forward[0].att_o,
            att1_h=forward[1].att_o,
            branch0_h=ends[0].branch_o,
            branch1_h=ends[1].branch_o,
        ),
        dict(
            x=narrow_all,
            dq=narrow,
            pair=pair_all,
            att=narrow,
            branch=narrow,
            turn=turn,
            turn_all=turn_all,
        ),
        (steps[last][0],),
    )
    away, total = first_sums(
        (fence(self_halves[0], one_own[1], one_own[-1], steps[last][1]), self_halves[1])
    )
    self_total = middle_sums((away, total))
    one_own = jnp.stack([one_own[0]] + [fence(part, self_total) for part in one_own[1:]])
    self_share = last_sums((self_total,))
    one_own_x = send(fence(one_own, self_total), to_x)

    early = sum(end.gain_early_o[0] for end in ends)
    late = jnp.where(
        decoder,
        sum(call.gain_grads_o[0] for call in cross),
        sum(call.gain_late_o[0] for call in feeds),
    )
    two_own = jnp.stack(
        gather_z(jnp.concatenate([self_share, gain_block([early, late])]))
    )
    two_own_x = send(fence(two_own, one_own_x), to_x)

    def columns(block):
        return pl.ds(block * width, width)

    def one_targets(r, block, row, rows):
        lines = pl.ds(row, rows)
        feed = [r.up_o.at[lines, columns(block)], r.down_o.at[pl.ds(block * width + row, rows)]]
        if block >= 2:
            return feed + [r.pair_o.at[lines, columns(block - 2)]]
        return feed + [(r.out_o if block else r.query_o).at[lines]]

    def two_targets(r, block, row, rows):
        lines = pl.ds(row, rows)
        return [r.out_o.at[lines] if block == 3 else r.mixed_o.at[lines, columns(block)]]

    square_out = ((width, width), f32)
    one_own_x = fence(one_own_x, two_own)
    one_grads = spread(
        one_targets,
        one_own,
        one_own_x,
        dict(
            up_o=((width, hidden), f32),
            query_o=square_out,
            pair_o=((width, 2 * width), f32),
            down_o=((hidden, width), f32),
            out_o=square_out,
            gains_o=((1, width), f32),
        ),
        3,
    )
    two_own_x = fence(two_own_x, one_grads.gains_o)
    two_grads = spread(
        two_targets,
        two_own,
        two_own_x,
        dict(
            mixed_o=((width, 3 * width), f32),
            out_o=square_out,
            gains_o=((2, width), f32),
        ),
        1,
    )

    grad_input = jnp.stack([step[1] for step in steps])
    return (
        results[None, :, None],
        grad_input.astype(f32)[None, :, None],
        two_grads.mixed_o[None],
        two_grads.out_o[None],
        one_grads.up_o[None],
        one_grads.down_o[None],
        two_grads.gains_o[None],
        one_grads.query_o,
        one_grads.pair_o,
        one_grads.out_o,
        one_grads.gains_o[0],
    )


def shards(*arrays):
    layer_input = arrays[0]
    micros, rows, length = layer_input.shape[1:4]
    simple = (
        lax.axis_size("section") == 2
        and lax.axis_size("seq") == 2
        and lax.axis_size("dp") in (4, 8, 16)
        and (micros, rows) == (2, 1)
        and length == layer_input.shape[-1] == CHUNK
        and arrays[4].shape[-1] == 4 * CHUNK
    )
    return split_rows(*arrays) if simple else any_rows(*arrays)


def solution(mesh):
    in_specs = (
        P("section", None, "dp", "seq", None),
        P("section", None, "dp", "seq"),
        P("section", None, None),
        P("section", None, None),
        P("section", None, None),
        P("section", None, None),
        P("section", None, None),
        P(),
        P(),
        P(),
        P(),
        P(None, "dp", "seq", None),
    )
    out_specs = (
        P("section", None, "dp", "seq", None),
        P("section", None, "dp", "seq", None),
        P("section", None, None),
        P("section", None, None),
        P("section", None, None),
        P("section", None, None),
        P("section", None, None),
        P(),
        P(),
        P(),
        P(),
    )
    return jax.shard_map(shards, mesh=mesh, in_specs=in_specs, out_specs=out_specs, check_vma=False)
```

profile of v0, /device:TPU:5, one launch (start us, length us, event | category | flops | bytes accessed | tf_op | source)
XLA Modules:
  0.0 376.5 jit_solution(2043059995083174666)
XLA Ops:
  3.0 3.7 collective-permute-start
  6.6 7.0 %collective-permute-done.refs_2_.refs_3_.refs_1_ = bf16[528,512]{1,0:T(8,128)(2,1)S(1)} collective-permute-done((bf16[528,512]{1,0:T(8,128)(2,1)S(1)}, bf16[528,512]{1,0:T(8,128)(2,1)S(1)}, u32[]{:S(2)}, u32[]{:S(2)}) %collective-permute-start) | collective-permute-done | bytes 540704 | tf_op jit(solution)/shard_map/ppermute | solution.py:1240
  14.4 3.6 collective-permute-start.3
  18.8 15.9 %shard_map.203 = (bf16[512,512]{1,0:T(8,128)(2,1)}, bf16[1024,1024]{1,0:T(8,128)(2,1)}, bf16[512,512]{1,0:T(8,128)(2,1)}, f32[2,8,512]{2,1,0:T(8,128)}, f32[512,...) custom-call(s32[4]{0:T(128)} %pad_add_fusion.refs_0_, ...), custom_call_target="tpu_custom_call" | custom-call | flops 25999998976 | bytes 1048576 | tf_op jit(solution)/shard_map/pallas_call | solution.py:663
  36.2 1.9 collective-permute-start.6
  39.0 14.0 %shard_map.204 = (bf16[512,512]{1,0:T(8,128)(2,1)}, bf16[1024,1024]{1,0:T(8,128)(2,1)}, bf16[512,512]{1,0:T(8,128)(2,1)}, f32[2,8,512]{2,1,0:T(8,128)}, f32[512,...) custom-call(s32[4]{0:T(128)} %pad_add_fusion.refs_0_, ...), custom_call_target="tpu_custom_call" | custom-call | flops 25999998976 | bytes 1048576 | tf_op jit(solution)/shard_map/pallas_call | solution.py:663
  56.0 36.6 %shard_map.205 = (bf16[512,512]{1,0:T(8,128)(2,1)}, bf16[512,512]{1,0:T(8,128)(2,1)}, bf16[512,2048]{1,0:T(8,128)(2,1)}, bf16[512,512]{1,0:T(8,128)(2,1)}, bf16[...) custom-call(s32[4]{0:T(128)} %pad_add_fusion.refs_0_, ...), custom_call_target="tpu_custom_call", output_to_operand_aliasing={{1}: (14, {}), {2}: (15, {})} | custom-call | flops 44000002048 | bytes 1048576 | tf_op jit(solution)/shard_map/pallas_call | solution.py:663
  93.1 1.6 collective-permute-done.9
  98.3 29.4 %shard_map.206 = (bf16[512,512]{1,0:T(8,128)(2,1)}, bf16[512,512]{1,0:T(8,128)(2,1)}, bf16[512,2048]{1,0:T(8,128)(2,1)}, bf16[512,512]{1,0:T(8,128)(2,1)}, bf16[...) custom-call(s32[4]{0:T(128)} %pad_add_fusion.refs_0_, ...), custom_call_target="tpu_custom_call", output_to_operand_aliasing={{1}: (14, {}), {2}: (15, {})} | custom-call | flops 44000002048 | bytes 1048576 | tf_op jit(solution)/shard_map/pallas_call | solution.py:663
  127.7 6.0 %collective-permute-start.12 = (bf16[512,512]{1,0:T(8,128)(2,1)}, bf16[512,512]{1,0:T(8,128)(2,1)S(1)}, u32[]{:S(2)}, u32[]{:S(2)}) collective-permute-start(bf16[512,512]{1,0:T(8,128)(2,1)} %get-tuple-element.168), channel_id=1, source_target_pairs={{0,1},{1,0},{2,3},{3,2},{4,5},{5,4},{6,7},{7,6},{8,9},{9,8},{10,11... | collective-permute-start | bytes 1572872 | tf_op jit(solution)/shard_map/ppermute | solution.py:1240
  135.1 1.9 collective-permute-start.10
  137.3 2.1 collective-permute-start.14
  139.4 8.3 %shard_map.209 = (bf16[2,512,512]{2,1,0:T(8,128)(2,1)}, bf16[2,512,512]{2,1,0:T(8,128)(2,1)}) custom-call(s32[4]{0:T(128)} %pad_add_fusion.refs_0_, bf16[512,512]{1,0:T(8,128)(2,1)} %get-tuple-element.142.refs_7_.refs_1_, bf16[512,512]{1,0:T(8,128)(2,1)} %get-tuple-element.150.refs_7_.refs_2_, bf16[512,512]{1,0:T(8,128)(2,1)} %get-tuple-element.177.refs_3_, ...), custom_call_target="tpu_custom_call" | custom-call | flops 8000000000 | bytes 1048576 | tf_op jit(solution)/shard_map/pallas_call | solution.py:663
  147.7 1.9 collective-permute-start.13
  150.5 1.5 shard_map.208
  152.6 3.7 collective-permute-start.15
  156.3 22.4 %shard_map.210 = (bf16[512,512]{1,0:T(8,128)(2,1)}, bf16[1024,1024]{1,0:T(8,128)(2,1)}, f32[8,512]{1,0:T(8,128)}, bf16[512,512]{1,0:T(8,128)(2,1)}, f32[512,512]{1,0:T(8,128)}, /*index=5*/bf16[512,512]{1,0:T(8,128)(2,1)}) custom-call(s32[4]{0:T(128)} %pad_add_fusion.refs_0_, ...), custom_call_target="tpu_custom_call", output_to_operand_aliasing={{0}: (13, {}), {1}: (14, {}), {2}: (15, {}), {3}: (16, {}),... | custom-call | flops 22000001024 | bytes 1048576 | tf_op jit(solution)/shard_map/pallas_call | solution.py:663
  183.6 7.1 %shard_map.212 = (bf16[2,512,512]{2,1,0:T(8,128)(2,1)}, bf16[2,512,512]{2,1,0:T(8,128)(2,1)}) custom-call(s32[4]{0:T(128)} %pad_add_fusion.refs_0_, bf16[512,512]{1,0:T(8,128)(2,1)} %get-tuple-element.206.refs_1_, bf16[512,512]{1,0:T(8,128)(2,1)} %get-tuple-element.207.refs_2_, bf16[512,2048]{1,0:T(8,128)(2,1)} %get-tuple-element.208.refs_3_, ...), custom_call_target="tpu_custom_call" | custom-call | flops 8000000000 | bytes 1048576 | tf_op jit(solution)/shard_map/pallas_call | solution.py:663
  190.9 2.7 collective-permute-done.18
  194.8 2.2 collective-permute-start.19
  197.1 7.1 %shard_map.213 = (bf16[2,512,512]{2,1,0:T(8,128)(2,1)}, bf16[2,512,512]{2,1,0:T(8,128)(2,1)}) custom-call(s32[4]{0:T(128)} %pad_add_fusion.refs_0_, bf16[512,2048]{1,0:T(8,128)(2,1)} %get-tuple-element.202.refs_1_, bf16[512,2048]{1,0:T(8,128)(2,1)} %get-tuple-element.203.refs_2_, bf16[512,512]{1,0:T(8,128)(2,1)} %get-tuple-element.204.refs_3_, ...), custom_call_target="tpu_custom_call" | custom-call | flops 8000000000 | bytes 1048576 | tf_op jit(solution)/shard_map/pallas_call | solution.py:663
  204.2 5.1 %collective-permute-done.19 = bf16[512,512]{1,0:T(8,128)(2,1)S(1)} collective-permute-done((bf16[512,512]{1,0:T(8,128)(2,1)S(1)}, bf16[512,512]{1,0:T(8,128)(2,1)S(1)}, u32[]{:S(2)}, u32[]{:S(2)}) %collective-permute-start.19) | collective-permute-done | bytes 524320 | tf_op jit(solution)/shard_map/ppermute | solution.py:1240
  211.0 3.3 collective-permute-start.17
  214.5 2.3 collective-permute-start.21
  216.8 9.7 %collective-permute-start.22 = (bf16[256,512]{1,0:T(8,128)(2,1)S(1)}, bf16[256,512]{1,0:T(8,128)(2,1)S(1)}, u32[]{:S(2)}, u32[]{:S(2)}) collective-permute-start(bf16[256,512]{1,0:T(8,128)(2,1)S(1)} %get-tuple-element.274), channel_id=1, source_target_pairs={{0,4},{1,5},{2,6},{3,7},{4,0},{5,1},{6,2},{7,3},{8,12},{9,13},{10,... | collective-permute-start | bytes 786440 | tf_op jit(solution)/shard_map/ppermute | solution.py:1240
  228.5 10.6 %shard_map.214 = (bf16[512,512]{1,0:T(8,128)(2,1)}, bf16[1024,1024]{1,0:T(8,128)(2,1)}, f32[8,512]{1,0:T(8,128)}, bf16[512,512]{1,0:T(8,128)(2,1)}, f32[512,512]{1,0:T(8,128)}, /*index=5*/bf16[512,512]{1,0:T(8,128)(2,1)}) custom-call(s32[4]{0:T(128)} %pad_add_fusion.refs_0_, f32[2,512]{1,0:T(2,128)} %bitcast.142, bf16[528,512]{1,0:T(8,128)(2,1)} %copy-done.32, ...), custom_call_target="tpu_custom_call" | custom-call | flops 12000000000 | bytes 1048576 | tf_op jit(solution)/shard_map/pallas_call | solution.py:663
  239.1 5.2 %collective-permute-done.22 = bf16[256,512]{1,0:T(8,128)(2,1)S(1)} collective-permute-done((bf16[256,512]{1,0:T(8,128)(2,1)S(1)}, bf16[256,512]{1,0:T(8,128)(2,1)S(1)}, u32[]{:S(2)}, u32[]{:S(2)}) %collective-permute-start.22) | collective-permute-done | bytes 262176 | tf_op jit(solution)/shard_map/ppermute | solution.py:1240
  246.1 5.6 %collective-permute-start.27 = (bf16[128,512]{1,0:T(8,128)(2,1)S(1)}, bf16[128,512]{1,0:T(8,128)(2,1)S(1)}, u32[]{:S(2)}, u32[]{:S(2)}) collective-permute-start(bf16[128,512]{1,0:T(8,128)(2,1)S(1)} %get-tuple-element.282), channel_id=1, source_target_pairs={{0,6},{1,7},{2,0},{3,1},{4,2},{5,3},{6,4},{7,5},{8,14},{9,15},{10,... | collective-permute-start | bytes 393224 | tf_op jit(solution)/shard_map/ppermute | solution.py:1240
  251.7 1.5 collective-permute-start.26
  253.7 10.9 %shard_map.215 = (bf16[512,512]{1,0:T(8,128)(2,1)}, bf16[1024,1024]{1,0:T(8,128)(2,1)}, f32[512,512]{1,0:T(8,128)}, bf16[512,512]{1,0:T(8,128)(2,1)}) custom-call(s32[4]{0:T(128)} %pad_add_fusion.refs_0_, f32[2,512]{1,0:T(2,128)} %bitcast.143, bf16[528,512]{1,0:T(8,128)(2,1)} %copy-done.32, bf16[528,512]{1,0:T(8,128)(2,1)} %copy-done.33, ...), custom_call_target="tpu_custom_call" | custom-call | flops 12000000000 | bytes 1048576 | tf_op jit(solution)/shard_map/pallas_call | solution.py:663
  266.4 3.6 collective-permute-start.32
  270.2 2.2 collective-permute-start.30
  272.5 8.3 %shard_map.216 = (bf16[2,512,512]{2,1,0:T(8,128)(2,1)}, bf16[2,512,512]{2,1,0:T(8,128)(2,1)}) custom-call(s32[4]{0:T(128)} %pad_add_fusion.refs_0_, bf16[528,512]{1,0:T(8,128)(2,1)} %copy-done.30, bf16[528,512]{1,0:T(8,128)(2,1)} %copy-done.32, bf16[528,512]{1,0:T(8,128)(2,1)} %copy-done.31, bf16[528,512]{1,0:T(8,128)(2,1)} %copy-done.33, ...), custom_call_target="tpu_custom_call" | custom-call | flops 8000000000 | bytes 1048576 | tf_op jit(solution)/shard_map/pallas_call | solution.py:663
  280.8 7.4 %collective-permute-done.31 = bf16[400,512]{1,0:T(8,128)(2,1)S(1)} collective-permute-done((bf16[400,512]{1,0:T(8,128)(2,1)S(1)}, bf16[400,512]{1,0:T(8,128)(2,1)S(1)}, u32[]{:S(2)}, u32[]{:S(2)}) %collective-permute-start.31) | collective-permute-done | bytes 409632 | tf_op jit(solution)/shard_map/ppermute | solution.py:1240
  289.2 2.5 collective-permute-done.33
  293.9 12.2 %collective-permute-done.34 = bf16[512,512]{1,0:T(8,128)(2,1)S(1)} collective-permute-done((bf16[512,512]{1,0:T(8,128)(2,1)S(1)}, bf16[512,512]{1,0:T(8,128)(2,1)S(1)}, u32[]{:S(2)}, u32[]{:S(2)}) %collective-permute-start.34) | collective-permute-done | bytes 524320 | tf_op jit(solution)/shard_map/ppermute | solution.py:1240
  307.3 6.1 %collective-permute-done.41 = bf16[400,512]{1,0:T(8,128)(2,1)S(1)} collective-permute-done((bf16[400,512]{1,0:T(8,128)(2,1)S(1)}, bf16[400,512]{1,0:T(8,128)(2,1)S(1)}, u32[]{:S(2)}, u32[]{:S(2)}) %collective-permute-start.41) | collective-permute-done | bytes 409632 | tf_op jit(solution)/shard_map/ppermute | solution.py:1240
  314.9 3.3 collective-permute-start.37
  318.9 2.4 collective-permute-start.44
  321.3 7.8 %collective-permute-done.36 = bf16[128,512]{1,0:T(8,128)(2,1)S(1)} collective-permute-done((bf16[128,512]{1,0:T(8,128)(2,1)S(1)}, bf16[128,512]{1,0:T(8,128)(2,1)S(1)}, u32[]{:S(2)}, u32[]{:S(2)}) %collective-permute-start.36) | collective-permute-done | bytes 131104 | tf_op jit(solution)/shard_map/ppermute | solution.py:1240
  330.6 2.1 collective-permute-start.40
  332.8 8.2 %collective-permute-done.39 = bf16[144,512]{1,0:T(8,128)(2,1)S(1)} collective-permute-done((bf16[144,512]{1,0:T(8,128)(2,1)S(1)}, bf16[144,512]{1,0:T(8,128)(2,1)S(1)}, u32[]{:S(2)}, u32[]{:S(2)}) %collective-permute-start.39) | collective-permute-done | bytes 147488 | tf_op jit(solution)/shard_map/ppermute | solution.py:1240
  341.4 8.4 %collective-permute-done.42.refs_2_ = bf16[4,400,512]{2,1,0:T(8,128)(2,1)S(1)} collective-permute-done((bf16[4,400,512]{2,1,0:T(8,128)(2,1)S(1)}, bf16[4,400,512]{2,1,0:T(8,128)(2,1)S(1)}, u32[]{:S(2)}, u32[]{:S(2)}) %collective-permute-start.42) | collective-permute-done | bytes 1638432 | tf_op jit(solution)/shard_map/ppermute | solution.py:1240
  349.8 2.1 collective-permute-start.45
  355.2 7.9 %shard_map.217 = (f32[512,2048]{1,0:T(8,128)}, f32[512,512]{1,0:T(8,128)}, f32[512,1024]{1,0:T(8,128)}, f32[2048,512]{1,0:T(8,128)}, f32[512,512]{1,0:T(8,128)}, /*index=5*/f32[1,512]{1,0:T(1,128)}) custom-call(s32[4]{0:T(128)} %pad_add_fusion.refs_0_, bf16[4,400,512]{2,1,0:T(8,128)(2,1)} %copy-done.1, bf16[4,400,512]{2,1,0:T(8,128)(2,1)} %copy-done.23, ...), custom_call_target="tpu_custom_call" | custom-call | flops 5000000000 | bytes 1048576 | tf_op jit(solution)/shard_map/pallas_call | solution.py:663
  363.1 3.8 %collective-permute-done.43.refs_2_ = bf16[4,144,512]{2,1,0:T(8,128)(2,1)S(1)} collective-permute-done((bf16[4,144,512]{2,1,0:T(8,128)(2,1)S(1)}, bf16[4,144,512]{2,1,0:T(8,128)(2,1)S(1)}, u32[]{:S(2)}, u32[]{:S(2)}) %collective-permute-start.43) | collective-permute-done | bytes 589856 | tf_op jit(solution)/shard_map/ppermute | solution.py:1240
  367.6 1.5 maximum_convert_fusion
  370.7 4.6 %shard_map.218 = (f32[512,1536]{1,0:T(8,128)}, f32[512,512]{1,0:T(8,128)}, f32[2,512]{1,0:T(2,128)}) custom-call(s32[4]{0:T(128)} %pad_add_fusion.refs_0_, bf16[4,144,512]{2,1,0:T(8,128)(2,1)} %copy-done.11, bf16[4,144,512]{2,1,0:T(8,128)(2,1)} %copy-done.27, bf16[4,144,512]{2,1,0:T(8,128)(2,1)} %copy-done.28, bf16[4,144,512]{2,1,0:T(8,128)(2,1)} %copy-done.29), custom_call_target="tpu_custom_call" | custom-call | flops 5000000000 | bytes 1048576 | tf_op jit(solution)/shard_map/pallas_call | solution.py:663
  (186 shorter events, 45.5 us)
Async XLA Ops:
  3.0 10.7 %collective-permute-start = (bf16[528,512]{1,0:T(8,128)(2,1)S(1)}, bf16[528,512]{1,0:T(8,128)(2,1)S(1)}, u32[]{:S(2)}, u32[]{:S(2)}) collective-permute-start(bf16[528,512]{1,0:T(8,128)(2,1)S(1)} %get-tuple-element.293), channel_id=1, source_target_pairs={{0,0},{1,8},{2,2},{3,10},{4,4},{5,12},{6,6},{7,14},{8,1},{9,9},{10... | collective-permute-start | bytes 1622024 | tf_op jit(solution)/shard_map/ppermute | solution.py:1240
  13.7 4.3 %collective-permute-start.1 = (bf16[528,512]{1,0:T(8,128)(2,1)S(1)}, bf16[528,512]{1,0:T(8,128)(2,1)S(1)}, u32[]{:S(2)}, u32[]{:S(2)}) collective-permute-start(bf16[528,512]{1,0:T(8,128)(2,1)S(1)} %collective-permute-done.refs_2_.refs_3_.refs_1_), channel_id=1, source_target_pairs={{0,1},{1,0},{2,3},{3,2},{4,5},{5,4},{6,7},{7,6},{8,9},{9,8},{10,11... | collective-permute-start | bytes 1622024 | tf_op jit(solution)/shard_map/ppermute | solution.py:1240
  14.4 20.4 %collective-permute-start.3 = (bf16[528,512]{1,0:T(8,128)(2,1)S(1)}, bf16[528,512]{1,0:T(8,128)(2,1)S(1)}, u32[]{:S(2)}, u32[]{:S(2)}) collective-permute-start(bf16[528,512]{1,0:T(8,128)(2,1)S(1)} %get-tuple-element.137), channel_id=1, source_target_pairs={{0,0},{1,8},{2,2},{3,10},{4,4},{5,12},{6,6},{7,14},{8,1},{9,9},{10... | collective-permute-start | bytes 1622024 | tf_op jit(solution)/shard_map/ppermute | solution.py:1240
  34.8 3.3 collective-permute-start.4
  34.9 18.1 %collective-permute-start.2 = (bf16[528,512]{1,0:T(8,128)(2,1)}, bf16[528,512]{1,0:T(8,128)(2,1)S(1)}, u32[]{:S(2)}, u32[]{:S(2)}) collective-permute-start(bf16[528,512]{1,0:T(8,128)(2,1)} %get-tuple-element.136), channel_id=1, source_target_pairs={{0,16},{1,17},{2,18},{3,19},{4,20},{5,21},{6,22},{7,23},{8,24},{9,... | collective-permute-start | bytes 1622024 | tf_op jit(solution)/shard_map/ppermute | solution.py:1240
  36.2 18.6 %collective-permute-start.6 = (bf16[2,512,512]{2,1,0:T(8,128)(2,1)S(1)}, bf16[2,512,512]{2,1,0:T(8,128)(2,1)S(1)}, u32[]{:S(2)}, u32[]{:S(2)}) collective-permute-start(bf16[2,512,512]{2,1,0:T(8,128)(2,1)S(1)} %bitcast.128), channel_id=1, source_target_pairs={{0,0},{1,8},{2,2},{3,10},{4,4},{5,12},{6,6},{7,14},{8,1},{9,9},{10... | collective-permute-start | bytes 3145736 | tf_op jit(solution)/shard_map/ppermute | solution.py:1240
  53.0 2.1 collective-permute-start.5
  53.5 39.4 %collective-permute-start.7 = (bf16[528,512]{1,0:T(8,128)(2,1)}, bf16[528,512]{1,0:T(8,128)(2,1)S(1)}, u32[]{:S(2)}, u32[]{:S(2)}) collective-permute-start(bf16[528,512]{1,0:T(8,128)(2,1)} %get-tuple-element.148), channel_id=1, source_target_pairs={{0,16},{1,17},{2,18},{3,19},{4,20},{5,21},{6,22},{7,23},{8,24},{9,... | collective-permute-start | bytes 1622024 | tf_op jit(solution)/shard_map/ppermute | solution.py:1240
  92.6 2.2 collective-permute-start.9
  92.9 4.6 %collective-permute-start.8 = (bf16[528,512]{1,0:T(8,128)(2,1)S(1)}, bf16[528,512]{1,0:T(8,128)(2,1)S(1)}, u32[]{:S(2)}, u32[]{:S(2)}) collective-permute-start(bf16[528,512]{1,0:T(8,128)(2,1)S(1)} %collective-permute-done.7.refs_4_.refs_10_), channel_id=1, source_target_pairs={{0,1},{1,0},{2,3},{3,2},{4,5},{5,4},{6,7},{7,6},{8,9},{9,8},{10,11... | collective-permute-start | bytes 1622024 | tf_op jit(solution)/shard_map/ppermute | solution.py:1240
  96.1 31.6 %collective-permute-start.11 = (bf16[512,512]{1,0:T(8,128)(2,1)S(1)}, bf16[512,512]{1,0:T(8,128)(2,1)S(1)}, u32[]{:S(2)}, u32[]{:S(2)}) collective-permute-start(bf16[512,512]{1,0:T(8,128)(2,1)S(1)} %add_convert_fusion.7.refs_16_), channel_id=1, source_target_pairs={{16,0},{17,1},{18,2},{19,3},{20,4},{21,5},{22,6},{23,7},{24,8},{25... | collective-permute-start | bytes 1572872 | tf_op jit(solution)/shard_map/ppermute | solution.py:1240
  127.7 9.3 %collective-permute-start.12 = (bf16[512,512]{1,0:T(8,128)(2,1)}, bf16[512,512]{1,0:T(8,128)(2,1)S(1)}, u32[]{:S(2)}, u32[]{:S(2)}) collective-permute-start(bf16[512,512]{1,0:T(8,128)(2,1)} %get-tuple-element.168), channel_id=1, source_target_pairs={{0,1},{1,0},{2,3},{3,2},{4,5},{5,4},{6,7},{7,6},{8,9},{9,8},{10,11... | collective-permute-start | bytes 1572872 | tf_op jit(solution)/shard_map/ppermute | solution.py:1240
  135.1 47.5 %collective-permute-start.10 = (bf16[2,512,512]{2,1,0:T(8,128)(2,1)S(1)}, bf16[2,512,512]{2,1,0:T(8,128)(2,1)S(1)}, u32[]{:S(2)}, u32[]{:S(2)}) collective-permute-start(bf16[2,512,512]{2,1,0:T(8,128)(2,1)S(1)} %pad_maximum_fusion.1), channel_id=1, source_target_pairs={{0,0},{1,8},{2,2},{3,10},{4,4},{5,12},{6,6},{7,14},{8,1},{9,9},{10... | collective-permute-start | bytes 3145736 | tf_op jit(solution)/shard_map/ppermute | solution.py:1240
  137.3 19.0 %collective-permute-start.14 = (bf16[512,512]{1,0:T(8,128)(2,1)S(1)}, bf16[512,512]{1,0:T(8,128)(2,1)}, u32[]{:S(2)}, u32[]{:S(2)}) collective-permute-start(bf16[512,512]{1,0:T(8,128)(2,1)S(1)} %add_convert_fusion.6.refs_11_.refs_15_), channel_id=1, source_target_pairs={{16,0},{17,1},{18,2},{19,3},{20,4},{21,5},{22,6},{23,7},{24,8},{25... | collective-permute-start | bytes 1572872 | tf_op jit(solution)/shard_map/ppermute | solution.py:1240
  147.7 4.8 %collective-permute-start.13 = (bf16[2,512,512]{2,1,0:T(8,128)(2,1)}, bf16[2,512,512]{2,1,0:T(8,128)(2,1)S(1)}, u32[]{:S(2)}, u32[]{:S(2)}) collective-permute-start(bf16[2,512,512]{2,1,0:T(8,128)(2,1)} %get-tuple-element.186), channel_id=1, source_target_pairs={{16,17},{17,16},{18,19},{19,18},{20,21},{21,20},{22,23},{23,22},{2... | collective-permute-start | bytes 3145736 | tf_op jit(solution)/shard_map/ppermute | solution.py:1240
  152.6 26.2 %collective-permute-start.15 = (bf16[512,512]{1,0:T(8,128)(2,1)S(1)}, bf16[512,512]{1,0:T(8,128)(2,1)S(1)}, u32[]{:S(2)}, u32[]{:S(2)}) collective-permute-start(bf16[512,512]{1,0:T(8,128)(2,1)S(1)} %fusion.4.refs_19_), channel_id=1, source_target_pairs={{16,24},{17,25},{18,26},{19,27},{20,28},{21,29},{22,30},{23,31},{2... | collective-permute-start | bytes 1572872 | tf_op jit(solution)/shard_map/ppermute | solution.py:1240
  179.8 1.9 collective-permute-start.16
  190.7 2.9 collective-permute-start.18
  194.8 14.4 %collective-permute-start.19 = (bf16[512,512]{1,0:T(8,128)(2,1)S(1)}, bf16[512,512]{1,0:T(8,128)(2,1)S(1)}, u32[]{:S(2)}, u32[]{:S(2)}) collective-permute-start(bf16[512,512]{1,0:T(8,128)(2,1)S(1)} %fusion.5.refs_5_), channel_id=1, source_target_pairs={{0,8},{1,9},{2,10},{3,11},{4,12},{5,13},{6,14},{7,15},{8,0},{9,1},... | collective-permute-start | bytes 1572872 | tf_op jit(solution)/shard_map/ppermute | solution.py:1240
  209.4 18.1 %collective-permute-start.20 = (bf16[2,512,512]{2,1,0:T(8,128)(2,1)}, bf16[2,512,512]{2,1,0:T(8,128)(2,1)S(1)}, u32[]{:S(2)}, u32[]{:S(2)}) collective-permute-start(bf16[2,512,512]{2,1,0:T(8,128)(2,1)} %get-tuple-element.214), channel_id=1, source_target_pairs={{0,1},{1,0},{2,3},{3,2},{4,5},{5,4},{6,7},{7,6},{8,9},{9,8},{10,11... | collective-permute-start | bytes 3145736 | tf_op jit(solution)/shard_map/ppermute | solution.py:1240
  211.0 53.9 %collective-permute-start.17 = (bf16[512,512]{1,0:T(8,128)(2,1)}, bf16[512,512]{1,0:T(8,128)(2,1)S(1)}, u32[]{:S(2)}, u32[]{:S(2)}) collective-permute-start(bf16[512,512]{1,0:T(8,128)(2,1)} %add_convert_fusion.4.refs_6_), channel_id=1, source_target_pairs={{0,0},{1,8},{2,2},{3,10},{4,4},{5,12},{6,6},{7,14},{8,1},{9,9},{10... | collective-permute-start | bytes 1572872 | tf_op jit(solution)/shard_map/ppermute | solution.py:1240
  214.5 29.8 %collective-permute-start.21 = (bf16[256,512]{1,0:T(8,128)(2,1)S(1)}, bf16[256,512]{1,0:T(8,128)(2,1)S(1)}, u32[]{:S(2)}, u32[]{:S(2)}) collective-permute-start(bf16[256,512]{1,0:T(8,128)(2,1)S(1)} %get-tuple-element.273), channel_id=1, source_target_pairs={{0,2},{1,3},{2,4},{3,5},{4,6},{5,7},{6,0},{7,1},{8,10},{9,11},{10,... | collective-permute-start | bytes 786440 | tf_op jit(solution)/shard_map/ppermute | solution.py:1240
  216.8 27.5 %collective-permute-start.22 = (bf16[256,512]{1,0:T(8,128)(2,1)S(1)}, bf16[256,512]{1,0:T(8,128)(2,1)S(1)}, u32[]{:S(2)}, u32[]{:S(2)}) collective-permute-start(bf16[256,512]{1,0:T(8,128)(2,1)S(1)} %get-tuple-element.274), channel_id=1, source_target_pairs={{0,4},{1,5},{2,6},{3,7},{4,0},{5,1},{6,2},{7,3},{8,12},{9,13},{10,... | collective-permute-start | bytes 786440 | tf_op jit(solution)/shard_map/ppermute | solution.py:1240
  226.5 12.6 %collective-permute-start.23 = (bf16[256,512]{1,0:T(8,128)(2,1)S(1)}, bf16[256,512]{1,0:T(8,128)(2,1)S(1)}, u32[]{:S(2)}, u32[]{:S(2)}) collective-permute-start(bf16[256,512]{1,0:T(8,128)(2,1)S(1)} %get-tuple-element.275), channel_id=1, source_target_pairs={{0,6},{1,7},{2,0},{3,1},{4,2},{5,3},{6,4},{7,5},{8,14},{9,15},{10,... | collective-permute-start | bytes 786440 | tf_op jit(solution)/shard_map/ppermute | solution.py:1240
  227.7 18.1 %collective-permute-start.24 = (bf16[512,512]{1,0:T(8,128)(2,1)S(1)}, bf16[512,512]{1,0:T(8,128)(2,1)S(1)}, u32[]{:S(2)}, u32[]{:S(2)}) collective-permute-start(bf16[512,512]{1,0:T(8,128)(2,1)S(1)} %fusion.6.refs_12_), channel_id=1, source_target_pairs={{0,8},{1,9},{2,10},{3,11},{4,12},{5,13},{6,14},{7,15},{8,0},{9,1},... | collective-permute-start | bytes 1572872 | tf_op jit(solution)/shard_map/ppermute | solution.py:1240
  244.5 20.5 %collective-permute-start.28 = (bf16[144,512]{1,0:T(8,128)(2,1)S(1)}, bf16[144,512]{1,0:T(8,128)(2,1)S(1)}, u32[]{:S(2)}, u32[]{:S(2)}) collective-permute-start(bf16[144,512]{1,0:T(8,128)(2,1)S(1)} %fusion.20), channel_id=1, source_target_pairs={{16,0},{17,1},{18,2},{19,3},{20,4},{21,5},{22,6},{23,7},{24,8},{25... | collective-permute-start | bytes 442376 | tf_op jit(solution)/shard_map/ppermute | solution.py:1240
  246.1 18.5 %collective-permute-start.27 = (bf16[128,512]{1,0:T(8,128)(2,1)S(1)}, bf16[128,512]{1,0:T(8,128)(2,1)S(1)}, u32[]{:S(2)}, u32[]{:S(2)}) collective-permute-start(bf16[128,512]{1,0:T(8,128)(2,1)S(1)} %get-tuple-element.282), channel_id=1, source_target_pairs={{0,6},{1,7},{2,0},{3,1},{4,2},{5,3},{6,4},{7,5},{8,14},{9,15},{10,... | collective-permute-start | bytes 393224 | tf_op jit(solution)/shard_map/ppermute | solution.py:1240
  251.7 13.2 %collective-permute-start.26 = (bf16[128,512]{1,0:T(8,128)(2,1)S(1)}, bf16[128,512]{1,0:T(8,128)(2,1)S(1)}, u32[]{:S(2)}, u32[]{:S(2)}) collective-permute-start(bf16[128,512]{1,0:T(8,128)(2,1)S(1)} %get-tuple-element.283), channel_id=1, source_target_pairs={{0,4},{1,5},{2,6},{3,7},{4,0},{5,1},{6,2},{7,3},{8,12},{9,13},{10,... | collective-permute-start | bytes 393224 | tf_op jit(solution)/shard_map/ppermute | solution.py:1240
  253.2 11.6 %collective-permute-start.25 = (bf16[128,512]{1,0:T(8,128)(2,1)S(1)}, bf16[128,512]{1,0:T(8,128)(2,1)S(1)}, u32[]{:S(2)}, u32[]{:S(2)}) collective-permute-start(bf16[128,512]{1,0:T(8,128)(2,1)S(1)} %get-tuple-element.284), channel_id=1, source_target_pairs={{0,2},{1,3},{2,4},{3,5},{4,6},{5,7},{6,0},{7,1},{8,10},{9,11},{10,... | collective-permute-start | bytes 393224 | tf_op jit(solution)/shard_map/ppermute | solution.py:1240
  265.0 5.1 %collective-permute-start.29 = (bf16[512,512]{1,0:T(8,128)(2,1)}, bf16[512,512]{1,0:T(8,128)(2,1)S(1)}, u32[]{:S(2)}, u32[]{:S(2)}) collective-permute-start(bf16[512,512]{1,0:T(8,128)(2,1)} %get-tuple-element.232), channel_id=1, source_target_pairs={{0,1},{1,0},{2,3},{3,2},{4,5},{5,4},{6,7},{7,6},{8,9},{9,8},{10,11... | collective-permute-start | bytes 1572872 | tf_op jit(solution)/shard_map/ppermute | solution.py:1240
  266.4 14.4 %collective-permute-start.32 = (bf16[400,512]{1,0:T(8,128)(2,1)S(1)}, bf16[400,512]{1,0:T(8,128)(2,1)S(1)}, u32[]{:S(2)}, u32[]{:S(2)}) collective-permute-start(bf16[400,512]{1,0:T(8,128)(2,1)S(1)} %get-tuple-element.286), channel_id=1, source_target_pairs={{0,6},{1,7},{2,0},{3,1},{4,2},{5,3},{6,4},{7,5},{8,14},{9,15},{10,... | collective-permute-start | bytes 1228808 | tf_op jit(solution)/shard_map/ppermute | solution.py:1240
  270.0 18.2 %collective-permute-start.31 = (bf16[400,512]{1,0:T(8,128)(2,1)S(1)}, bf16[400,512]{1,0:T(8,128)(2,1)S(1)}, u32[]{:S(2)}, u32[]{:S(2)}) collective-permute-start(bf16[400,512]{1,0:T(8,128)(2,1)S(1)} %get-tuple-element.286), channel_id=1, source_target_pairs={{0,2},{1,3},{2,4},{3,5},{4,6},{5,7},{6,0},{7,1},{8,10},{9,11},{10,... | collective-permute-start | bytes 1228808 | tf_op jit(solution)/shard_map/ppermute | solution.py:1240
  270.2 18.0 %collective-permute-start.30 = (bf16[512,512]{1,0:T(8,128)(2,1)S(1)}, bf16[512,512]{1,0:T(8,128)(2,1)S(1)}, u32[]{:S(2)}, u32[]{:S(2)}) collective-permute-start(bf16[512,512]{1,0:T(8,128)(2,1)S(1)} %add_convert_fusion.1.refs_13_), channel_id=1, source_target_pairs={{0,0},{1,8},{2,2},{3,10},{4,4},{5,12},{6,6},{7,14},{8,1},{9,9},{10... | collective-permute-start | bytes 1572872 | tf_op jit(solution)/shard_map/ppermute | solution.py:1240
  288.2 3.5 collective-permute-start.33
  292.9 13.2 %collective-permute-start.34 = (bf16[512,512]{1,0:T(8,128)(2,1)S(1)}, bf16[512,512]{1,0:T(8,128)(2,1)S(1)}, u32[]{:S(2)}, u32[]{:S(2)}) collective-permute-start(bf16[512,512]{1,0:T(8,128)(2,1)S(1)} %fusion.7), channel_id=1, source_target_pairs={{0,8},{1,9},{2,10},{3,11},{4,12},{5,13},{6,14},{7,15},{8,0},{9,1},... | collective-permute-start | bytes 1572872 | tf_op jit(solution)/shard_map/ppermute | solution.py:1240
  293.0 20.4 %collective-permute-start.41 = (bf16[400,512]{1,0:T(8,128)(2,1)S(1)}, bf16[400,512]{1,0:T(8,128)(2,1)S(1)}, u32[]{:S(2)}, u32[]{:S(2)}) collective-permute-start(bf16[400,512]{1,0:T(8,128)(2,1)S(1)} %get-tuple-element.286), channel_id=1, source_target_pairs={{0,4},{1,5},{2,6},{3,7},{4,0},{5,1},{6,2},{7,3},{8,12},{9,13},{10,... | collective-permute-start | bytes 1228808 | tf_op jit(solution)/shard_map/ppermute | solution.py:1240
  313.6 36.2 %collective-permute-start.42 = (bf16[4,400,512]{2,1,0:T(8,128)(2,1)S(1)}, bf16[4,400,512]{2,1,0:T(8,128)(2,1)S(1)}, u32[]{:S(2)}, u32[]{:S(2)}) collective-permute-start(bf16[4,400,512]{2,1,0:T(8,128)(2,1)S(1)} %pad_maximum_fusion.refs_1_), channel_id=1, source_target_pairs={{0,8},{1,9},{2,10},{3,11},{4,12},{5,13},{6,14},{7,15},{8,0},{9,1},... | collective-permute-start | bytes 4915208 | tf_op jit(solution)/shard_map/ppermute | solution.py:1240
  314.9 6.4 %collective-permute-start.35 = (bf16[128,512]{1,0:T(8,128)(2,1)S(1)}, bf16[128,512]{1,0:T(8,128)(2,1)S(1)}, u32[]{:S(2)}, u32[]{:S(2)}) collective-permute-start(bf16[128,512]{1,0:T(8,128)(2,1)S(1)} %get-tuple-element.278), channel_id=1, source_target_pairs={{0,2},{1,3},{2,4},{3,5},{4,6},{5,7},{6,0},{7,1},{8,10},{9,11},{10,... | collective-permute-start | bytes 393224 | tf_op jit(solution)/shard_map/ppermute | solution.py:1240
  314.9 6.4 %collective-permute-start.37 = (bf16[128,512]{1,0:T(8,128)(2,1)S(1)}, bf16[128,512]{1,0:T(8,128)(2,1)S(1)}, u32[]{:S(2)}, u32[]{:S(2)}) collective-permute-start(bf16[128,512]{1,0:T(8,128)(2,1)S(1)} %get-tuple-element.279), channel_id=1, source_target_pairs={{0,6},{1,7},{2,0},{3,1},{4,2},{5,3},{6,4},{7,5},{8,14},{9,15},{10,... | collective-permute-start | bytes 393224 | tf_op jit(solution)/shard_map/ppermute | solution.py:1240
  318.2 10.9 %collective-permute-start.36 = (bf16[128,512]{1,0:T(8,128)(2,1)S(1)}, bf16[128,512]{1,0:T(8,128)(2,1)S(1)}, u32[]{:S(2)}, u32[]{:S(2)}) collective-permute-start(bf16[128,512]{1,0:T(8,128)(2,1)S(1)} %get-tuple-element.280), channel_id=1, source_target_pairs={{0,4},{1,5},{2,6},{3,7},{4,0},{5,1},{6,2},{7,3},{8,12},{9,13},{10,... | collective-permute-start | bytes 393224 | tf_op jit(solution)/shard_map/ppermute | solution.py:1240
  318.9 34.3 %collective-permute-start.44 = (bf16[4,400,512]{2,1,0:T(8,128)(2,1)S(1)}, bf16[4,400,512]{2,1,0:T(8,128)(2,1)S(1)}, u32[]{:S(2)}, u32[]{:S(2)}) collective-permute-start(bf16[4,400,512]{2,1,0:T(8,128)(2,1)S(1)} %pad_maximum_fusion.refs_1_), channel_id=1, source_target_pairs={{0,1},{1,0},{2,3},{3,2},{4,5},{5,4},{6,7},{7,6},{8,9},{9,8},{10,11... | collective-permute-start | bytes 4915208 | tf_op jit(solution)/shard_map/ppermute | solution.py:1240
  329.3 11.7 %collective-permute-start.39 = (bf16[144,512]{1,0:T(8,128)(2,1)S(1)}, bf16[144,512]{1,0:T(8,128)(2,1)S(1)}, u32[]{:S(2)}, u32[]{:S(2)}) collective-permute-start(bf16[144,512]{1,0:T(8,128)(2,1)S(1)} %maximum_maximum_fusion.2), channel_id=1, source_target_pairs={{0,4},{1,5},{2,6},{3,7},{4,0},{5,1},{6,2},{7,3},{8,12},{9,13},{10,... | collective-permute-start | bytes 442376 | tf_op jit(solution)/shard_map/ppermute | solution.py:1240
  329.4 11.6 %collective-permute-start.38 = (bf16[144,512]{1,0:T(8,128)(2,1)S(1)}, bf16[144,512]{1,0:T(8,128)(2,1)S(1)}, u32[]{:S(2)}, u32[]{:S(2)}) collective-permute-start(bf16[144,512]{1,0:T(8,128)(2,1)S(1)} %maximum_maximum_fusion.2), channel_id=1, source_target_pairs={{0,2},{1,3},{2,4},{3,5},{4,6},{5,7},{6,0},{7,1},{8,10},{9,11},{10,... | collective-permute-start | bytes 442376 | tf_op jit(solution)/shard_map/ppermute | solution.py:1240
  330.6 10.7 %collective-permute-start.40 = (bf16[144,512]{1,0:T(8,128)(2,1)S(1)}, bf16[144,512]{1,0:T(8,128)(2,1)S(1)}, u32[]{:S(2)}, u32[]{:S(2)}) collective-permute-start(bf16[144,512]{1,0:T(8,128)(2,1)S(1)} %maximum_maximum_fusion.2), channel_id=1, source_target_pairs={{0,6},{1,7},{2,0},{3,1},{4,2},{5,3},{6,4},{7,5},{8,14},{9,15},{10,... | collective-permute-start | bytes 442376 | tf_op jit(solution)/shard_map/ppermute | solution.py:1240
  349.8 5.4 %collective-permute-start.45 = (bf16[4,400,512]{2,1,0:T(8,128)(2,1)S(1)}, bf16[4,400,512]{2,1,0:T(8,128)(2,1)}, u32[]{:S(2)}, u32[]{:S(2)}) collective-permute-start(bf16[4,400,512]{2,1,0:T(8,128)(2,1)S(1)} %collective-permute-done.42.refs_2_), channel_id=1, source_target_pairs={{0,1},{1,0},{2,3},{3,2},{4,5},{5,4},{6,7},{7,6},{8,9},{9,8},{10,11... | collective-permute-start | bytes 4915208 | tf_op jit(solution)/shard_map/ppermute | solution.py:1240
  351.9 15.0 %collective-permute-start.43 = (bf16[4,144,512]{2,1,0:T(8,128)(2,1)S(1)}, bf16[4,144,512]{2,1,0:T(8,128)(2,1)S(1)}, u32[]{:S(2)}, u32[]{:S(2)}) collective-permute-start(bf16[4,144,512]{2,1,0:T(8,128)(2,1)S(1)} %pad_maximum_fusion.2.refs_1_), channel_id=1, source_target_pairs={{0,8},{1,9},{2,10},{3,11},{4,12},{5,13},{6,14},{7,15},{8,0},{9,1},... | collective-permute-start | bytes 1769480 | tf_op jit(solution)/shard_map/ppermute | solution.py:1240
  353.0 16.1 %collective-permute-start.46 = (bf16[4,144,512]{2,1,0:T(8,128)(2,1)S(1)}, bf16[4,144,512]{2,1,0:T(8,128)(2,1)S(1)}, u32[]{:S(2)}, u32[]{:S(2)}) collective-permute-start(bf16[4,144,512]{2,1,0:T(8,128)(2,1)S(1)} %pad_maximum_fusion.2.refs_1_), channel_id=1, source_target_pairs={{0,1},{1,0},{2,3},{3,2},{4,5},{5,4},{6,7},{7,6},{8,9},{9,8},{10,11... | collective-permute-start | bytes 1769480 | tf_op jit(solution)/shard_map/ppermute | solution.py:1240
  366.9 2.4 collective-permute-start.47
  (40 other events, 351.7 us)
where the time goes:
time: 383 us; the launch traced here: 376 us
  Pallas kernels  186 us (49%)
  starting transfers between devices  82.1 us (21%)
  waiting for transfers between devices  81.2 us (21%)
  other arithmetic  14 us (4%)
  local copies, waits for them, and re-layouts  11 us (3%)
    pallas_call x16, Pallas kernels, launch(): pl.pallas_call(body, out_shape=[jax.ShapeDtypeStruct(*shape) for shape in...  186 us
    ppermute x48, starting transfers between devices, send(): return lax.ppermute(values, axes, route)  82.1 us
    ppermute x48, waiting for transfers between devices, send(): return lax.ppermute(values, axes, route)  81.2 us
    unnamed x81, local copies, waits for them, and re-layouts  9.5 us
  transfers between devices with their start and end apart: 48, of which 20 were waited for; matrix products, arithmetic and copies ran while one was open for 3% of the time, Pallas kernels for 46%

commit v1 on v0

--- a/solution.py
+++ b/solution.py
@@ -1805,7 +1805,7 @@
         (steps[last][0],),
     )
     away, total = first_sums(
-        (fence(self_halves[0], one_own[1], one_own[-1], steps[last][1]), self_halves[1])
+        (fence(self_halves[0], one_own[1], steps[last][1]), self_halves[1])
     )
     self_total = middle_sums((away, total))
     one_own = jnp.stack([one_own[0]] + [fence(part, self_total) for part in one_own[1:]])

time: 383 us -> 383 us (level)
  Pallas kernels: 186 us -> 196 us
  starting transfers between devices: 82.1 us -> 74.1 us
    pallas_call x16, Pallas kernels: 186 us -> 196 us  [launch(): pl.pallas_call(body, out_shape=[jax.ShapeDtypeStruct(*shape) for shape in...]
    ppermute x48, starting transfers between devices: 82.1 us -> 74.1 us  [send(): return lax.ppermute(values, axes, route)]
  transfers between devices with their start and end apart: 48 -> 48, of which waited for: 20 -> 17; matrix products, arithmetic and copies ran while one was open for 3% -> 3% of each run, Pallas kernels for 46% -> 49%
where the time goes in v1:
time: 383 us; the launch traced here: 375 us
  Pallas kernels  196 us (51%)
  waiting for transfers between devices  77.9 us (20%)
  starting transfers between devices  74.1 us (19%)
  other arithmetic  14.1 us (4%)
  local copies, waits for them, and re-layouts  11.5 us (3%)
    pallas_call x16, Pallas kernels, launch(): pl.pallas_call(body, out_shape=[jax.ShapeDtypeStruct(*shape) for shape in...  196 us
    ppermute x48, waiting for transfers between devices, send(): return lax.ppermute(values, axes, route)  77.9 us
    ppermute x48, starting transfers between devices, send(): return lax.ppermute(values, axes, route)  74.1 us
    unnamed x81, local copies, waits for them, and re-layouts  9.99 us
  transfers between devices with their start and end apart: 48, of which 17 were waited for; matrix products, arithmetic and copies ran while one was open for 3% of the time, Pallas kernels for 49%

profile of v1, /device:TPU:5, one launch (start us, length us, event | category | flops | bytes accessed | tf_op | source)
XLA Modules:
  0.0 375.4 jit_solution(13799498595701922396)
XLA Ops:
  3.0 3.7 collective-permute-start
  6.6 7.0 %collective-permute-done.refs_2_.refs_3_.refs_1_ = bf16[528,512]{1,0:T(8,128)(2,1)S(1)} collective-permute-done((bf16[528,512]{1,0:T(8,128)(2,1)S(1)}, bf16[528,512]{1,0:T(8,128)(2,1)S(1)}, u32[]{:S(2)}, u32[]{:S(2)}) %collective-permute-start) | collective-permute-done | bytes 540704 | tf_op jit(solution)/shard_map/ppermute | solution.py:1240
  14.4 3.6 collective-permute-start.3
  18.8 15.9 %shard_map.203 = (bf16[512,512]{1,0:T(8,128)(2,1)}, bf16[1024,1024]{1,0:T(8,128)(2,1)}, bf16[512,512]{1,0:T(8,128)(2,1)}, f32[2,8,512]{2,1,0:T(8,128)}, f32[512,...) custom-call(s32[4]{0:T(128)} %pad_add_fusion.refs_0_, ...), custom_call_target="tpu_custom_call" | custom-call | flops 25999998976 | bytes 1048576 | tf_op jit(solution)/shard_map/pallas_call | solution.py:663
  36.2 1.9 collective-permute-start.6
  39.0 15.5 %shard_map.204 = (bf16[512,512]{1,0:T(8,128)(2,1)}, bf16[1024,1024]{1,0:T(8,128)(2,1)}, bf16[512,512]{1,0:T(8,128)(2,1)}, f32[2,8,512]{2,1,0:T(8,128)}, f32[512,...) custom-call(s32[4]{0:T(128)} %pad_add_fusion.refs_0_, ...), custom_call_target="tpu_custom_call" | custom-call | flops 25999998976 | bytes 1048576 | tf_op jit(solution)/shard_map/pallas_call | solution.py:663
  57.3 36.6 %shard_map.205 = (bf16[512,512]{1,0:T(8,128)(2,1)}, bf16[512,512]{1,0:T(8,128)(2,1)}, bf16[512,2048]{1,0:T(8,128)(2,1)}, bf16[512,512]{1,0:T(8,128)(2,1)}, bf16[...) custom-call(s32[4]{0:T(128)} %pad_add_fusion.refs_0_, ...), custom_call_target="tpu_custom_call", output_to_operand_aliasing={{1}: (14, {}), {2}: (15, {})} | custom-call | flops 44000002048 | bytes 1048576 | tf_op jit(solution)/shard_map/pallas_call | solution.py:663
  94.5 1.6 collective-permute-done.9
  96.1 1.4 add_convert_fusion.7.refs_16_
  99.7 35.8 %shard_map.206 = (bf16[512,512]{1,0:T(8,128)(2,1)}, bf16[512,512]{1,0:T(8,128)(2,1)}, bf16[512,2048]{1,0:T(8,128)(2,1)}, bf16[512,512]{1,0:T(8,128)(2,1)}, bf16[...) custom-call(s32[4]{0:T(128)} %pad_add_fusion.refs_0_, ...), custom_call_target="tpu_custom_call", output_to_operand_aliasing={{1}: (14, {}), {2}: (15, {})} | custom-call | flops 44000002048 | bytes 1048576 | tf_op jit(solution)/shard_map/pallas_call | solution.py:663
  137.0 1.9 collective-permute-start.10
  139.1 2.1 collective-permute-start.14
  141.2 8.3 %shard_map.209 = (bf16[2,512,512]{2,1,0:T(8,128)(2,1)}, bf16[2,512,512]{2,1,0:T(8,128)(2,1)}) custom-call(s32[4]{0:T(128)} %pad_add_fusion.refs_0_, bf16[512,512]{1,0:T(8,128)(2,1)} %get-tuple-element.142.refs_7_.refs_1_, bf16[512,512]{1,0:T(8,128)(2,1)} %get-tuple-element.150.refs_7_.refs_2_, bf16[512,512]{1,0:T(8,128)(2,1)} %get-tuple-element.177.refs_3_, ...), custom_call_target="tpu_custom_call" | custom-call | flops 8000000000 | bytes 1048576 | tf_op jit(solution)/shard_map/pallas_call | solution.py:663
  149.5 1.9 collective-permute-start.13
  152.3 1.5 shard_map.208
  154.4 3.7 collective-permute-start.15
  158.1 22.4 %shard_map.210 = (bf16[512,512]{1,0:T(8,128)(2,1)}, bf16[1024,1024]{1,0:T(8,128)(2,1)}, f32[8,512]{1,0:T(8,128)}, bf16[512,512]{1,0:T(8,128)(2,1)}, f32[512,512]{1,0:T(8,128)}, /*index=5*/bf16[512,512]{1,0:T(8,128)(2,1)}) custom-call(s32[4]{0:T(128)} %pad_add_fusion.refs_0_, ...), custom_call_target="tpu_custom_call", output_to_operand_aliasing={{0}: (13, {}), {1}: (14, {}), {2}: (15, {}), {3}: (16, {}),... | custom-call | flops 22000001024 | bytes 1048576 | tf_op jit(solution)/shard_map/pallas_call | solution.py:663
  185.4 7.1 %shard_map.212 = (bf16[2,512,512]{2,1,0:T(8,128)(2,1)}, bf16[2,512,512]{2,1,0:T(8,128)(2,1)}) custom-call(s32[4]{0:T(128)} %pad_add_fusion.refs_0_, bf16[512,512]{1,0:T(8,128)(2,1)} %get-tuple-element.206.refs_1_, bf16[512,512]{1,0:T(8,128)(2,1)} %get-tuple-element.207.refs_2_, bf16[512,2048]{1,0:T(8,128)(2,1)} %get-tuple-element.208.refs_3_, ...), custom_call_target="tpu_custom_call" | custom-call | flops 8000000000 | bytes 1048576 | tf_op jit(solution)/shard_map/pallas_call | solution.py:663
  192.7 2.7 collective-permute-done.18
  197.4 7.1 %shard_map.213 = (bf16[2,512,512]{2,1,0:T(8,128)(2,1)}, bf16[2,512,512]{2,1,0:T(8,128)(2,1)}) custom-call(s32[4]{0:T(128)} %pad_add_fusion.refs_0_, bf16[512,2048]{1,0:T(8,128)(2,1)} %get-tuple-element.202.refs_1_, bf16[512,2048]{1,0:T(8,128)(2,1)} %get-tuple-element.203.refs_2_, bf16[512,512]{1,0:T(8,128)(2,1)} %get-tuple-element.204.refs_3_, ...), custom_call_target="tpu_custom_call" | custom-call | flops 8000000000 | bytes 1048576 | tf_op jit(solution)/shard_map/pallas_call | solution.py:663
  204.5 5.6 %collective-permute-done.19 = bf16[512,512]{1,0:T(8,128)(2,1)S(1)} collective-permute-done((bf16[512,512]{1,0:T(8,128)(2,1)S(1)}, bf16[512,512]{1,0:T(8,128)(2,1)S(1)}, u32[]{:S(2)}, u32[]{:S(2)}) %collective-permute-start.19) | collective-permute-done | bytes 524320 | tf_op jit(solution)/shard_map/ppermute | solution.py:1240
  212.1 2.0 collective-permute-start.17
  214.2 3.1 collective-permute-start.21
  217.3 5.7 %collective-permute-start.22 = (bf16[256,512]{1,0:T(8,128)(2,1)S(1)}, bf16[256,512]{1,0:T(8,128)(2,1)S(1)}, u32[]{:S(2)}, u32[]{:S(2)}) collective-permute-start(bf16[256,512]{1,0:T(8,128)(2,1)S(1)} %get-tuple-element.274), channel_id=1, source_target_pairs={{0,4},{1,5},{2,6},{3,7},{4,0},{5,1},{6,2},{7,3},{8,12},{9,13},{10,... | collective-permute-start | bytes 786440 | tf_op jit(solution)/shard_map/ppermute | solution.py:1240
  223.0 2.3 collective-permute-start.23
  226.3 11.6 %shard_map.214 = (bf16[512,512]{1,0:T(8,128)(2,1)}, bf16[1024,1024]{1,0:T(8,128)(2,1)}, f32[8,512]{1,0:T(8,128)}, bf16[512,512]{1,0:T(8,128)(2,1)}, f32[512,512]{1,0:T(8,128)}, /*index=5*/bf16[512,512]{1,0:T(8,128)(2,1)}) custom-call(s32[4]{0:T(128)} %pad_add_fusion.refs_0_, f32[2,512]{1,0:T(2,128)} %bitcast.142, bf16[528,512]{1,0:T(8,128)(2,1)} %copy-done.32, ...), custom_call_target="tpu_custom_call" | custom-call | flops 12000000000 | bytes 1048576 | tf_op jit(solution)/shard_map/pallas_call | solution.py:663
  239.7 10.5 %collective-permute-start.27 = (bf16[128,512]{1,0:T(8,128)(2,1)S(1)}, bf16[128,512]{1,0:T(8,128)(2,1)S(1)}, u32[]{:S(2)}, u32[]{:S(2)}) collective-permute-start(bf16[128,512]{1,0:T(8,128)(2,1)S(1)} %get-tuple-element.282), channel_id=1, source_target_pairs={{0,6},{1,7},{2,0},{3,1},{4,2},{5,3},{6,4},{7,5},{8,14},{9,15},{10,... | collective-permute-start | bytes 393224 | tf_op jit(solution)/shard_map/ppermute | solution.py:1240
  251.0 11.8 %shard_map.215 = (bf16[512,512]{1,0:T(8,128)(2,1)}, bf16[1024,1024]{1,0:T(8,128)(2,1)}, f32[512,512]{1,0:T(8,128)}, bf16[512,512]{1,0:T(8,128)(2,1)}) custom-call(s32[4]{0:T(128)} %pad_add_fusion.refs_0_, f32[2,512]{1,0:T(2,128)} %bitcast.143, bf16[528,512]{1,0:T(8,128)(2,1)} %copy-done.32, bf16[528,512]{1,0:T(8,128)(2,1)} %copy-done.33, ...), custom_call_target="tpu_custom_call" | custom-call | flops 12000000000 | bytes 1048576 | tf_op jit(solution)/shard_map/pallas_call | solution.py:663
  263.1 3.2 collective-permute-start.31
  266.5 2.8 collective-permute-start.30
  269.3 8.3 %shard_map.216 = (bf16[2,512,512]{2,1,0:T(8,128)(2,1)}, bf16[2,512,512]{2,1,0:T(8,128)(2,1)}) custom-call(s32[4]{0:T(128)} %pad_add_fusion.refs_0_, bf16[528,512]{1,0:T(8,128)(2,1)} %copy-done.30, bf16[528,512]{1,0:T(8,128)(2,1)} %copy-done.32, bf16[528,512]{1,0:T(8,128)(2,1)} %copy-done.31, bf16[528,512]{1,0:T(8,128)(2,1)} %copy-done.33, ...), custom_call_target="tpu_custom_call" | custom-call | flops 8000000000 | bytes 1048576 | tf_op jit(solution)/shard_map/pallas_call | solution.py:663
  277.8 2.9 collective-permute-done.32
  282.8 2.6 collective-permute-start.41
  285.9 9.4 %collective-permute-done.33 = bf16[512,512]{1,0:T(8,128)(2,1)S(1)} collective-permute-done((bf16[512,512]{1,0:T(8,128)(2,1)S(1)}, bf16[512,512]{1,0:T(8,128)(2,1)S(1)}, u32[]{:S(2)}, u32[]{:S(2)}) %collective-permute-start.33) | collective-permute-done | bytes 524320 | tf_op jit(solution)/shard_map/ppermute | solution.py:1240
  296.5 15.8 %collective-permute-done.40 = bf16[400,512]{1,0:T(8,128)(2,1)S(1)} collective-permute-done((bf16[400,512]{1,0:T(8,128)(2,1)S(1)}, bf16[400,512]{1,0:T(8,128)(2,1)S(1)}, u32[]{:S(2)}, u32[]{:S(2)}) %collective-permute-start.40) | collective-permute-done | bytes 409632 | tf_op jit(solution)/shard_map/ppermute | solution.py:1240
  313.2 3.3 collective-permute-start.36
  317.2 2.0 collective-permute-start.44
  319.2 8.0 %collective-permute-done.35 = bf16[128,512]{1,0:T(8,128)(2,1)S(1)} collective-permute-done((bf16[128,512]{1,0:T(8,128)(2,1)S(1)}, bf16[128,512]{1,0:T(8,128)(2,1)S(1)}, u32[]{:S(2)}, u32[]{:S(2)}) %collective-permute-start.35) | collective-permute-done | bytes 131104 | tf_op jit(solution)/shard_map/ppermute | solution.py:1240
  327.5 1.3 collective-permute-start.37
  328.9 2.0 collective-permute-start.39
  330.9 8.3 %collective-permute-done.38 = bf16[144,512]{1,0:T(8,128)(2,1)S(1)} collective-permute-done((bf16[144,512]{1,0:T(8,128)(2,1)S(1)}, bf16[144,512]{1,0:T(8,128)(2,1)S(1)}, u32[]{:S(2)}, u32[]{:S(2)}) %collective-permute-start.38) | collective-permute-done | bytes 147488 | tf_op jit(solution)/shard_map/ppermute | solution.py:1240
  339.8 8.6 %collective-permute-done.42.refs_2_ = bf16[4,400,512]{2,1,0:T(8,128)(2,1)S(1)} collective-permute-done((bf16[4,400,512]{2,1,0:T(8,128)(2,1)S(1)}, bf16[4,400,512]{2,1,0:T(8,128)(2,1)S(1)}, u32[]{:S(2)}, u32[]{:S(2)}) %collective-permute-start.42) | collective-permute-done | bytes 1638432 | tf_op jit(solution)/shard_map/ppermute | solution.py:1240
  348.4 2.4 collective-permute-start.45
  352.7 1.4 collective-permute-done.45.refs_4_
  354.1 7.9 %shard_map.217 = (f32[512,2048]{1,0:T(8,128)}, f32[512,512]{1,0:T(8,128)}, f32[512,1024]{1,0:T(8,128)}, f32[2048,512]{1,0:T(8,128)}, f32[512,512]{1,0:T(8,128)}, /*index=5*/f32[1,512]{1,0:T(1,128)}) custom-call(s32[4]{0:T(128)} %pad_add_fusion.refs_0_, bf16[4,400,512]{2,1,0:T(8,128)(2,1)} %copy-done.1, bf16[4,400,512]{2,1,0:T(8,128)(2,1)} %copy-done.23, ...), custom_call_target="tpu_custom_call" | custom-call | flops 5000000000 | bytes 1048576 | tf_op jit(solution)/shard_map/pallas_call | solution.py:663
  362.0 3.8 %collective-permute-done.43.refs_2_ = bf16[4,144,512]{2,1,0:T(8,128)(2,1)S(1)} collective-permute-done((bf16[4,144,512]{2,1,0:T(8,128)(2,1)S(1)}, bf16[4,144,512]{2,1,0:T(8,128)(2,1)S(1)}, u32[]{:S(2)}, u32[]{:S(2)}) %collective-permute-start.43) | collective-permute-done | bytes 589856 | tf_op jit(solution)/shard_map/ppermute | solution.py:1240
  366.6 1.5 maximum_convert_fusion
  369.7 4.6 %shard_map.218 = (f32[512,1536]{1,0:T(8,128)}, f32[512,512]{1,0:T(8,128)}, f32[2,512]{1,0:T(2,128)}) custom-call(s32[4]{0:T(128)} %pad_add_fusion.refs_0_, bf16[4,144,512]{2,1,0:T(8,128)(2,1)} %copy-done.11, bf16[4,144,512]{2,1,0:T(8,128)(2,1)} %copy-done.27, bf16[4,144,512]{2,1,0:T(8,128)(2,1)} %copy-done.28, bf16[4,144,512]{2,1,0:T(8,128)(2,1)} %copy-done.29), custom_call_target="tpu_custom_call" | custom-call | flops 5000000000 | bytes 1048576 | tf_op jit(solution)/shard_map/pallas_call | solution.py:663
  (186 shorter events, 39.2 us)
Async XLA Ops:
  3.0 10.7 %collective-permute-start = (bf16[528,512]{1,0:T(8,128)(2,1)S(1)}, bf16[528,512]{1,0:T(8,128)(2,1)S(1)}, u32[]{:S(2)}, u32[]{:S(2)}) collective-permute-start(bf16[528,512]{1,0:T(8,128)(2,1)S(1)} %get-tuple-element.293), channel_id=1, source_target_pairs={{0,0},{1,8},{2,2},{3,10},{4,4},{5,12},{6,6},{7,14},{8,1},{9,9},{10... | collective-permute-start | bytes 1622024 | tf_op jit(solution)/shard_map/ppermute | solution.py:1240
  13.7 4.3 %collective-permute-start.1 = (bf16[528,512]{1,0:T(8,128)(2,1)S(1)}, bf16[528,512]{1,0:T(8,128)(2,1)S(1)}, u32[]{:S(2)}, u32[]{:S(2)}) collective-permute-start(bf16[528,512]{1,0:T(8,128)(2,1)S(1)} %collective-permute-done.refs_2_.refs_3_.refs_1_), channel_id=1, source_target_pairs={{0,1},{1,0},{2,3},{3,2},{4,5},{5,4},{6,7},{7,6},{8,9},{9,8},{10,11... | collective-permute-start | bytes 1622024 | tf_op jit(solution)/shard_map/ppermute | solution.py:1240
  14.4 20.4 %collective-permute-start.3 = (bf16[528,512]{1,0:T(8,128)(2,1)S(1)}, bf16[528,512]{1,0:T(8,128)(2,1)S(1)}, u32[]{:S(2)}, u32[]{:S(2)}) collective-permute-start(bf16[528,512]{1,0:T(8,128)(2,1)S(1)} %get-tuple-element.137), channel_id=1, source_target_pairs={{0,0},{1,8},{2,2},{3,10},{4,4},{5,12},{6,6},{7,14},{8,1},{9,9},{10... | collective-permute-start | bytes 1622024 | tf_op jit(solution)/shard_map/ppermute | solution.py:1240
  34.8 3.3 collective-permute-start.4
  34.9 19.6 %collective-permute-start.2 = (bf16[528,512]{1,0:T(8,128)(2,1)}, bf16[528,512]{1,0:T(8,128)(2,1)S(1)}, u32[]{:S(2)}, u32[]{:S(2)}) collective-permute-start(bf16[528,512]{1,0:T(8,128)(2,1)} %get-tuple-element.136), channel_id=1, source_target_pairs={{0,16},{1,17},{2,18},{3,19},{4,20},{5,21},{6,22},{7,23},{8,24},{9,... | collective-permute-start | bytes 1622024 | tf_op jit(solution)/shard_map/ppermute | solution.py:1240
  36.2 19.7 %collective-permute-start.6 = (bf16[2,512,512]{2,1,0:T(8,128)(2,1)S(1)}, bf16[2,512,512]{2,1,0:T(8,128)(2,1)S(1)}, u32[]{:S(2)}, u32[]{:S(2)}) collective-permute-start(bf16[2,512,512]{2,1,0:T(8,128)(2,1)S(1)} %bitcast.128), channel_id=1, source_target_pairs={{0,0},{1,8},{2,2},{3,10},{4,4},{5,12},{6,6},{7,14},{8,1},{9,9},{10... | collective-permute-start | bytes 3145736 | tf_op jit(solution)/shard_map/ppermute | solution.py:1240
  54.5 2.0 collective-permute-start.5
  54.6 39.6 %collective-permute-start.7 = (bf16[528,512]{1,0:T(8,128)(2,1)}, bf16[528,512]{1,0:T(8,128)(2,1)S(1)}, u32[]{:S(2)}, u32[]{:S(2)}) collective-permute-start(bf16[528,512]{1,0:T(8,128)(2,1)} %get-tuple-element.148), channel_id=1, source_target_pairs={{0,16},{1,17},{2,18},{3,19},{4,20},{5,21},{6,22},{7,23},{8,24},{9,... | collective-permute-start | bytes 1622024 | tf_op jit(solution)/shard_map/ppermute | solution.py:1240
  93.9 2.2 collective-permute-start.9
  94.2 4.6 %collective-permute-start.8 = (bf16[528,512]{1,0:T(8,128)(2,1)S(1)}, bf16[528,512]{1,0:T(8,128)(2,1)S(1)}, u32[]{:S(2)}, u32[]{:S(2)}) collective-permute-start(bf16[528,512]{1,0:T(8,128)(2,1)S(1)} %collective-permute-done.7.refs_4_.refs_10_), channel_id=1, source_target_pairs={{0,1},{1,0},{2,3},{3,2},{4,5},{5,4},{6,7},{7,6},{8,9},{9,8},{10,11... | collective-permute-start | bytes 1622024 | tf_op jit(solution)/shard_map/ppermute | solution.py:1240
  97.5 37.9 %collective-permute-start.11 = (bf16[512,512]{1,0:T(8,128)(2,1)S(1)}, bf16[512,512]{1,0:T(8,128)(2,1)S(1)}, u32[]{:S(2)}, u32[]{:S(2)}) collective-permute-start(bf16[512,512]{1,0:T(8,128)(2,1)S(1)} %add_convert_fusion.7.refs_16_), channel_id=1, source_target_pairs={{16,0},{17,1},{18,2},{19,3},{20,4},{21,5},{22,6},{23,7},{24,8},{25... | collective-permute-start | bytes 1572872 | tf_op jit(solution)/shard_map/ppermute | solution.py:1240
  135.5 3.4 collective-permute-start.12
  137.0 47.5 %collective-permute-start.10 = (bf16[2,512,512]{2,1,0:T(8,128)(2,1)S(1)}, bf16[2,512,512]{2,1,0:T(8,128)(2,1)S(1)}, u32[]{:S(2)}, u32[]{:S(2)}) collective-permute-start(bf16[2,512,512]{2,1,0:T(8,128)(2,1)S(1)} %pad_maximum_fusion.1), channel_id=1, source_target_pairs={{0,0},{1,8},{2,2},{3,10},{4,4},{5,12},{6,6},{7,14},{8,1},{9,9},{10... | collective-permute-start | bytes 3145736 | tf_op jit(solution)/shard_map/ppermute | solution.py:1240
  139.1 19.0 %collective-permute-start.14 = (bf16[512,512]{1,0:T(8,128)(2,1)S(1)}, bf16[512,512]{1,0:T(8,128)(2,1)}, u32[]{:S(2)}, u32[]{:S(2)}) collective-permute-start(bf16[512,512]{1,0:T(8,128)(2,1)S(1)} %add_convert_fusion.6.refs_11_.refs_15_), channel_id=1, source_target_pairs={{16,0},{17,1},{18,2},{19,3},{20,4},{21,5},{22,6},{23,7},{24,8},{25... | collective-permute-start | bytes 1572872 | tf_op jit(solution)/shard_map/ppermute | solution.py:1240
  149.5 4.8 %collective-permute-start.13 = (bf16[2,512,512]{2,1,0:T(8,128)(2,1)}, bf16[2,512,512]{2,1,0:T(8,128)(2,1)S(1)}, u32[]{:S(2)}, u32[]{:S(2)}) collective-permute-start(bf16[2,512,512]{2,1,0:T(8,128)(2,1)} %get-tuple-element.186), channel_id=1, source_target_pairs={{16,17},{17,16},{18,19},{19,18},{20,21},{21,20},{22,23},{23,22},{2... | collective-permute-start | bytes 3145736 | tf_op jit(solution)/shard_map/ppermute | solution.py:1240
  154.4 26.2 %collective-permute-start.15 = (bf16[512,512]{1,0:T(8,128)(2,1)S(1)}, bf16[512,512]{1,0:T(8,128)(2,1)S(1)}, u32[]{:S(2)}, u32[]{:S(2)}) collective-permute-start(bf16[512,512]{1,0:T(8,128)(2,1)S(1)} %fusion.4.refs_19_), channel_id=1, source_target_pairs={{16,24},{17,25},{18,26},{19,27},{20,28},{21,29},{22,30},{23,31},{2... | collective-permute-start | bytes 1572872 | tf_op jit(solution)/shard_map/ppermute | solution.py:1240
  181.6 1.9 collective-permute-start.16
  192.5 2.9 collective-permute-start.18
  196.6 13.4 %collective-permute-start.19 = (bf16[512,512]{1,0:T(8,128)(2,1)S(1)}, bf16[512,512]{1,0:T(8,128)(2,1)S(1)}, u32[]{:S(2)}, u32[]{:S(2)}) collective-permute-start(bf16[512,512]{1,0:T(8,128)(2,1)S(1)} %fusion.5.refs_5_), channel_id=1, source_target_pairs={{0,8},{1,9},{2,10},{3,11},{4,12},{5,13},{6,14},{7,15},{8,0},{9,1},... | collective-permute-start | bytes 1572872 | tf_op jit(solution)/shard_map/ppermute | solution.py:1240
  210.3 15.0 %collective-permute-start.20 = (bf16[2,512,512]{2,1,0:T(8,128)(2,1)}, bf16[2,512,512]{2,1,0:T(8,128)(2,1)S(1)}, u32[]{:S(2)}, u32[]{:S(2)}) collective-permute-start(bf16[2,512,512]{2,1,0:T(8,128)(2,1)} %get-tuple-element.214), channel_id=1, source_target_pairs={{0,1},{1,0},{2,3},{3,2},{4,5},{5,4},{6,7},{7,6},{8,9},{9,8},{10,11... | collective-permute-start | bytes 3145736 | tf_op jit(solution)/shard_map/ppermute | solution.py:1240
  212.1 50.8 %collective-permute-start.17 = (bf16[512,512]{1,0:T(8,128)(2,1)}, bf16[512,512]{1,0:T(8,128)(2,1)S(1)}, u32[]{:S(2)}, u32[]{:S(2)}) collective-permute-start(bf16[512,512]{1,0:T(8,128)(2,1)} %add_convert_fusion.4.refs_6_), channel_id=1, source_target_pairs={{0,0},{1,8},{2,2},{3,10},{4,4},{5,12},{6,6},{7,14},{8,1},{9,9},{10... | collective-permute-start | bytes 1572872 | tf_op jit(solution)/shard_map/ppermute | solution.py:1240
  214.2 23.6 %collective-permute-start.21 = (bf16[256,512]{1,0:T(8,128)(2,1)S(1)}, bf16[256,512]{1,0:T(8,128)(2,1)S(1)}, u32[]{:S(2)}, u32[]{:S(2)}) collective-permute-start(bf16[256,512]{1,0:T(8,128)(2,1)S(1)} %get-tuple-element.273), channel_id=1, source_target_pairs={{0,2},{1,3},{2,4},{3,5},{4,6},{5,7},{6,0},{7,1},{8,10},{9,11},{10,... | collective-permute-start | bytes 786440 | tf_op jit(solution)/shard_map/ppermute | solution.py:1240
  217.3 20.5 %collective-permute-start.22 = (bf16[256,512]{1,0:T(8,128)(2,1)S(1)}, bf16[256,512]{1,0:T(8,128)(2,1)S(1)}, u32[]{:S(2)}, u32[]{:S(2)}) collective-permute-start(bf16[256,512]{1,0:T(8,128)(2,1)S(1)} %get-tuple-element.274), channel_id=1, source_target_pairs={{0,4},{1,5},{2,6},{3,7},{4,0},{5,1},{6,2},{7,3},{8,12},{9,13},{10,... | collective-permute-start | bytes 786440 | tf_op jit(solution)/shard_map/ppermute | solution.py:1240
  223.0 14.8 %collective-permute-start.23 = (bf16[256,512]{1,0:T(8,128)(2,1)S(1)}, bf16[256,512]{1,0:T(8,128)(2,1)S(1)}, u32[]{:S(2)}, u32[]{:S(2)}) collective-permute-start(bf16[256,512]{1,0:T(8,128)(2,1)S(1)} %get-tuple-element.275), channel_id=1, source_target_pairs={{0,6},{1,7},{2,0},{3,1},{4,2},{5,3},{6,4},{7,5},{8,14},{9,15},{10,... | collective-permute-start | bytes 786440 | tf_op jit(solution)/shard_map/ppermute | solution.py:1240
  225.5 13.9 %collective-permute-start.24 = (bf16[512,512]{1,0:T(8,128)(2,1)S(1)}, bf16[512,512]{1,0:T(8,128)(2,1)S(1)}, u32[]{:S(2)}, u32[]{:S(2)}) collective-permute-start(bf16[512,512]{1,0:T(8,128)(2,1)S(1)} %fusion.6.refs_12_), channel_id=1, source_target_pairs={{0,8},{1,9},{2,10},{3,11},{4,12},{5,13},{6,14},{7,15},{8,0},{9,1},... | collective-permute-start | bytes 1572872 | tf_op jit(solution)/shard_map/ppermute | solution.py:1240
  238.1 24.9 %collective-permute-start.28 = (bf16[144,512]{1,0:T(8,128)(2,1)S(1)}, bf16[144,512]{1,0:T(8,128)(2,1)S(1)}, u32[]{:S(2)}, u32[]{:S(2)}) collective-permute-start(bf16[144,512]{1,0:T(8,128)(2,1)S(1)} %fusion.20), channel_id=1, source_target_pairs={{16,0},{17,1},{18,2},{19,3},{20,4},{21,5},{22,6},{23,7},{24,8},{25... | collective-permute-start | bytes 442376 | tf_op jit(solution)/shard_map/ppermute | solution.py:1240
  239.7 23.1 %collective-permute-start.27 = (bf16[128,512]{1,0:T(8,128)(2,1)S(1)}, bf16[128,512]{1,0:T(8,128)(2,1)S(1)}, u32[]{:S(2)}, u32[]{:S(2)}) collective-permute-start(bf16[128,512]{1,0:T(8,128)(2,1)S(1)} %get-tuple-element.282), channel_id=1, source_target_pairs={{0,6},{1,7},{2,0},{3,1},{4,2},{5,3},{6,4},{7,5},{8,14},{9,15},{10,... | collective-permute-start | bytes 393224 | tf_op jit(solution)/shard_map/ppermute | solution.py:1240
  250.2 12.6 %collective-permute-start.26 = (bf16[128,512]{1,0:T(8,128)(2,1)S(1)}, bf16[128,512]{1,0:T(8,128)(2,1)S(1)}, u32[]{:S(2)}, u32[]{:S(2)}) collective-permute-start(bf16[128,512]{1,0:T(8,128)(2,1)S(1)} %get-tuple-element.283), channel_id=1, source_target_pairs={{0,4},{1,5},{2,6},{3,7},{4,0},{5,1},{6,2},{7,3},{8,12},{9,13},{10,... | collective-permute-start | bytes 393224 | tf_op jit(solution)/shard_map/ppermute | solution.py:1240
  250.2 12.6 %collective-permute-start.25 = (bf16[128,512]{1,0:T(8,128)(2,1)S(1)}, bf16[128,512]{1,0:T(8,128)(2,1)S(1)}, u32[]{:S(2)}, u32[]{:S(2)}) collective-permute-start(bf16[128,512]{1,0:T(8,128)(2,1)S(1)} %get-tuple-element.284), channel_id=1, source_target_pairs={{0,2},{1,3},{2,4},{3,5},{4,6},{5,7},{6,0},{7,1},{8,10},{9,11},{10,... | collective-permute-start | bytes 393224 | tf_op jit(solution)/shard_map/ppermute | solution.py:1240
  263.0 3.4 collective-permute-start.29
  263.1 14.5 %collective-permute-start.31 = (bf16[400,512]{1,0:T(8,128)(2,1)S(1)}, bf16[400,512]{1,0:T(8,128)(2,1)S(1)}, u32[]{:S(2)}, u32[]{:S(2)}) collective-permute-start(bf16[400,512]{1,0:T(8,128)(2,1)S(1)} %get-tuple-element.286), channel_id=1, source_target_pairs={{0,2},{1,3},{2,4},{3,5},{4,6},{5,7},{6,0},{7,1},{8,10},{9,11},{10,... | collective-permute-start | bytes 1228808 | tf_op jit(solution)/shard_map/ppermute | solution.py:1240
  266.5 11.1 %collective-permute-start.30 = (bf16[512,512]{1,0:T(8,128)(2,1)S(1)}, bf16[512,512]{1,0:T(8,128)(2,1)S(1)}, u32[]{:S(2)}, u32[]{:S(2)}) collective-permute-start(bf16[512,512]{1,0:T(8,128)(2,1)S(1)} %add_convert_fusion.1.refs_13_), channel_id=1, source_target_pairs={{0,0},{1,8},{2,2},{3,10},{4,4},{5,12},{6,6},{7,14},{8,1},{9,9},{10... | collective-permute-start | bytes 1572872 | tf_op jit(solution)/shard_map/ppermute | solution.py:1240
  277.7 2.9 collective-permute-start.32
  281.8 13.4 %collective-permute-start.33 = (bf16[512,512]{1,0:T(8,128)(2,1)S(1)}, bf16[512,512]{1,0:T(8,128)(2,1)S(1)}, u32[]{:S(2)}, u32[]{:S(2)}) collective-permute-start(bf16[512,512]{1,0:T(8,128)(2,1)S(1)} %fusion.7), channel_id=1, source_target_pairs={{0,8},{1,9},{2,10},{3,11},{4,12},{5,13},{6,14},{7,15},{8,0},{9,1},... | collective-permute-start | bytes 1572872 | tf_op jit(solution)/shard_map/ppermute | solution.py:1240
  282.8 13.7 %collective-permute-start.41 = (bf16[400,512]{1,0:T(8,128)(2,1)S(1)}, bf16[400,512]{1,0:T(8,128)(2,1)S(1)}, u32[]{:S(2)}, u32[]{:S(2)}) collective-permute-start(bf16[400,512]{1,0:T(8,128)(2,1)S(1)} %get-tuple-element.286), channel_id=1, source_target_pairs={{0,6},{1,7},{2,0},{3,1},{4,2},{5,3},{6,4},{7,5},{8,14},{9,15},{10,... | collective-permute-start | bytes 1228808 | tf_op jit(solution)/shard_map/ppermute | solution.py:1240
  285.3 27.0 %collective-permute-start.40 = (bf16[400,512]{1,0:T(8,128)(2,1)S(1)}, bf16[400,512]{1,0:T(8,128)(2,1)S(1)}, u32[]{:S(2)}, u32[]{:S(2)}) collective-permute-start(bf16[400,512]{1,0:T(8,128)(2,1)S(1)} %get-tuple-element.286), channel_id=1, source_target_pairs={{0,4},{1,5},{2,6},{3,7},{4,0},{5,1},{6,2},{7,3},{8,12},{9,13},{10,... | collective-permute-start | bytes 1228808 | tf_op jit(solution)/shard_map/ppermute | solution.py:1240
  312.6 35.8 %collective-permute-start.42 = (bf16[4,400,512]{2,1,0:T(8,128)(2,1)S(1)}, bf16[4,400,512]{2,1,0:T(8,128)(2,1)S(1)}, u32[]{:S(2)}, u32[]{:S(2)}) collective-permute-start(bf16[4,400,512]{2,1,0:T(8,128)(2,1)S(1)} %pad_maximum_fusion.refs_1_), channel_id=1, source_target_pairs={{0,8},{1,9},{2,10},{3,11},{4,12},{5,13},{6,14},{7,15},{8,0},{9,1},... | collective-permute-start | bytes 4915208 | tf_op jit(solution)/shard_map/ppermute | solution.py:1240
  313.1 6.1 %collective-permute-start.34 = (bf16[128,512]{1,0:T(8,128)(2,1)S(1)}, bf16[128,512]{1,0:T(8,128)(2,1)S(1)}, u32[]{:S(2)}, u32[]{:S(2)}) collective-permute-start(bf16[128,512]{1,0:T(8,128)(2,1)S(1)} %get-tuple-element.278), channel_id=1, source_target_pairs={{0,2},{1,3},{2,4},{3,5},{4,6},{5,7},{6,0},{7,1},{8,10},{9,11},{10,... | collective-permute-start | bytes 393224 | tf_op jit(solution)/shard_map/ppermute | solution.py:1240
  313.2 6.0 %collective-permute-start.36 = (bf16[128,512]{1,0:T(8,128)(2,1)S(1)}, bf16[128,512]{1,0:T(8,128)(2,1)S(1)}, u32[]{:S(2)}, u32[]{:S(2)}) collective-permute-start(bf16[128,512]{1,0:T(8,128)(2,1)S(1)} %get-tuple-element.279), channel_id=1, source_target_pairs={{0,6},{1,7},{2,0},{3,1},{4,2},{5,3},{6,4},{7,5},{8,14},{9,15},{10,... | collective-permute-start | bytes 393224 | tf_op jit(solution)/shard_map/ppermute | solution.py:1240
  316.4 10.8 %collective-permute-start.35 = (bf16[128,512]{1,0:T(8,128)(2,1)S(1)}, bf16[128,512]{1,0:T(8,128)(2,1)S(1)}, u32[]{:S(2)}, u32[]{:S(2)}) collective-permute-start(bf16[128,512]{1,0:T(8,128)(2,1)S(1)} %get-tuple-element.280), channel_id=1, source_target_pairs={{0,4},{1,5},{2,6},{3,7},{4,0},{5,1},{6,2},{7,3},{8,12},{9,13},{10,... | collective-permute-start | bytes 393224 | tf_op jit(solution)/shard_map/ppermute | solution.py:1240
  317.2 34.3 %collective-permute-start.44 = (bf16[4,400,512]{2,1,0:T(8,128)(2,1)S(1)}, bf16[4,400,512]{2,1,0:T(8,128)(2,1)S(1)}, u32[]{:S(2)}, u32[]{:S(2)}) collective-permute-start(bf16[4,400,512]{2,1,0:T(8,128)(2,1)S(1)} %pad_maximum_fusion.refs_1_), channel_id=1, source_target_pairs={{0,1},{1,0},{2,3},{3,2},{4,5},{5,4},{6,7},{7,6},{8,9},{9,8},{10,11... | collective-permute-start | bytes 4915208 | tf_op jit(solution)/shard_map/ppermute | solution.py:1240
  327.5 11.8 %collective-permute-start.38 = (bf16[144,512]{1,0:T(8,128)(2,1)S(1)}, bf16[144,512]{1,0:T(8,128)(2,1)S(1)}, u32[]{:S(2)}, u32[]{:S(2)}) collective-permute-start(bf16[144,512]{1,0:T(8,128)(2,1)S(1)} %maximum_maximum_fusion.2), channel_id=1, source_target_pairs={{0,4},{1,5},{2,6},{3,7},{4,0},{5,1},{6,2},{7,3},{8,12},{9,13},{10,... | collective-permute-start | bytes 442376 | tf_op jit(solution)/shard_map/ppermute | solution.py:1240
  327.5 11.7 %collective-permute-start.37 = (bf16[144,512]{1,0:T(8,128)(2,1)S(1)}, bf16[144,512]{1,0:T(8,128)(2,1)S(1)}, u32[]{:S(2)}, u32[]{:S(2)}) collective-permute-start(bf16[144,512]{1,0:T(8,128)(2,1)S(1)} %maximum_maximum_fusion.2), channel_id=1, source_target_pairs={{0,2},{1,3},{2,4},{3,5},{4,6},{5,7},{6,0},{7,1},{8,10},{9,11},{10,... | collective-permute-start | bytes 442376 | tf_op jit(solution)/shard_map/ppermute | solution.py:1240
  328.9 10.8 %collective-permute-start.39 = (bf16[144,512]{1,0:T(8,128)(2,1)S(1)}, bf16[144,512]{1,0:T(8,128)(2,1)S(1)}, u32[]{:S(2)}, u32[]{:S(2)}) collective-permute-start(bf16[144,512]{1,0:T(8,128)(2,1)S(1)} %maximum_maximum_fusion.2), channel_id=1, source_target_pairs={{0,6},{1,7},{2,0},{3,1},{4,2},{5,3},{6,4},{7,5},{8,14},{9,15},{10,... | collective-permute-start | bytes 442376 | tf_op jit(solution)/shard_map/ppermute | solution.py:1240
  348.4 5.7 %collective-permute-start.45 = (bf16[4,400,512]{2,1,0:T(8,128)(2,1)S(1)}, bf16[4,400,512]{2,1,0:T(8,128)(2,1)}, u32[]{:S(2)}, u32[]{:S(2)}) collective-permute-start(bf16[4,400,512]{2,1,0:T(8,128)(2,1)S(1)} %collective-permute-done.42.refs_2_), channel_id=1, source_target_pairs={{0,1},{1,0},{2,3},{3,2},{4,5},{5,4},{6,7},{7,6},{8,9},{9,8},{10,11... | collective-permute-start | bytes 4915208 | tf_op jit(solution)/shard_map/ppermute | solution.py:1240
  350.8 15.0 %collective-permute-start.43 = (bf16[4,144,512]{2,1,0:T(8,128)(2,1)S(1)}, bf16[4,144,512]{2,1,0:T(8,128)(2,1)S(1)}, u32[]{:S(2)}, u32[]{:S(2)}) collective-permute-start(bf16[4,144,512]{2,1,0:T(8,128)(2,1)S(1)} %pad_maximum_fusion.2.refs_1_), channel_id=1, source_target_pairs={{0,8},{1,9},{2,10},{3,11},{4,12},{5,13},{6,14},{7,15},{8,0},{9,1},... | collective-permute-start | bytes 1769480 | tf_op jit(solution)/shard_map/ppermute | solution.py:1240
  351.2 16.8 %collective-permute-start.46 = (bf16[4,144,512]{2,1,0:T(8,128)(2,1)S(1)}, bf16[4,144,512]{2,1,0:T(8,128)(2,1)S(1)}, u32[]{:S(2)}, u32[]{:S(2)}) collective-permute-start(bf16[4,144,512]{2,1,0:T(8,128)(2,1)S(1)} %pad_maximum_fusion.2.refs_1_), channel_id=1, source_target_pairs={{0,1},{1,0},{2,3},{3,2},{4,5},{5,4},{6,7},{7,6},{8,9},{9,8},{10,11... | collective-permute-start | bytes 1769480 | tf_op jit(solution)/shard_map/ppermute | solution.py:1240
  365.8 2.4 collective-permute-start.47
  (40 other events, 349.8 us)
